TPU v7x, 128 devices: a whole 4x4x4 slice. The times are simulated.
128 devices in a mesh: slab: 16 (over x, y_hi, core), cross: 8 (over y_lo, z).
Axes of the slice: x: 4, y: 4 (y_hi: 2, y_lo: 2; y = y_hi * 2 + y_lo), z: 4, core: 2. Of those that a mesh axis runs over, the one named last changes fastest.
Arguments:
- right_side: float32 [6, 6, 6, 16, 64, 128], P(None, None, None, 'slab', 'cross'), may hold values from -6 to 6
- coefficient: float32 [16, 64, 128], P('slab', 'cross'), may hold values from 0.3 to 3
- bottom_top: int32 [2, 16, 64], P(None, 'slab', 'cross'), may hold values 0 or 1
- stiff_five: float32 [216, 216], replicated, may hold values from -1 to 2
- stiff_three: float32 [64, 64], replicated, may hold values from -1 to 2
- stiff_one: float32 [8, 8], replicated, may hold values from -1 to 2
Outputs:
- solution: float32 [6, 6, 6, 16, 64, 128], P(None, None, None, 'slab', 'cross')
- residual: float32 [6, 6, 6, 16, 64, 128], P(None, None, None, 'slab', 'cross')
Inputs may be any that keep to these rules, and one draw needn't show every extreme that they name: `bottom_top`: 1 marks a face held at zero, 0 a face with no flux.
All inputs are finite; a program needn't handle non-finite values. No bound on the sum of `bottom_top` on one device may be relied on, other than what follows from the above.
Results may differ from a plain program's by a relative error of at most 0.00017.
Values sent between devices are 32-bit elements; how exact they have to be, the bound alone decides.
A program may use at most 128 MiB of HBM per device.

v0:
```python
import functools

import jax
import jax.numpy as jnp
import numpy as np
from jax import lax
from jax.experimental import pallas as pl
from jax.experimental.pallas import tpu as pltpu
from jax.sharding import PartitionSpec as P

MESH = pl.DeviceIdType.MESH
F32 = jnp.float32
BF16 = jnp.bfloat16
Q5, Q3, Q1 = 6, 4, 2
DEGREE = 3
COARSE_ITERS = 8
LAMBDA_TOP = 2.2
NY, NZ = 8, 128
PENALTY = {Q5: 3.0, Q3: 2.0, Q1: 1.0}


def lagrange(fine_count, coarse_count):
    fine = np.linspace(-1.0, 1.0, fine_count)
    coarse = np.linspace(-1.0, 1.0, coarse_count)
    table = np.ones((fine_count, coarse_count))
    for c in range(coarse_count):
        for o in range(coarse_count):
            if o != c:
                table[:, c] = table[:, c] * (fine - coarse[o]) / (coarse[c] - coarse[o])
    return table.astype(np.float32)


def chebyshev_factors(steps, lowest):
    center = 0.5 * (LAMBDA_TOP + lowest)
    radius = 0.5 * (LAMBDA_TOP - lowest)
    sigma = center / radius
    rho = 1.0 / sigma
    pairs = []
    for _ in range(steps - 1):
        rho_next = 1.0 / (2.0 * sigma - rho)
        pairs.append((rho_next * rho, 2.0 * rho_next / radius))
        rho = rho_next
    return 1.0 / center, pairs


def weighted(table_row, terms):
    total = None
    for value, term in zip(table_row, terms):
        if value == 0.0:
            continue
        part = term if value == 1.0 else float(value) * term
        total = part if total is None else total + part
    return total


def tiles(value, *lead):
    return value.reshape(*lead, NY, NZ)


def kernel(
    coef, ends, rhs, s5, s3, s1, sol, res,
    d5, t5, inv5, x3, r3, d3, t3, inv3, x1, r1, d1, t1, inv1,
    sh5, sl5, sh3, sl3, work, weights, hx, hy, ytile, pack, hc,
    ssem, rsem, csem, crsem,
):
    slab, cross = lax.axis_index("slab"), lax.axis_index("cross")
    ns, nc = lax.axis_size("slab"), lax.axis_size("cross")
    sides = (
        ("slab", slab - 1, slab > 0),
        ("slab", slab + 1, slab < ns - 1),
        ("cross", cross - 1, cross > 0),
        ("cross", cross + 1, cross < nc - 1),
    )
    hc[...] = jnp.zeros_like(hc)
    hx[...] = jnp.zeros_like(hx)
    hy[...] = jnp.zeros_like(hy)
    ytile[...] = jnp.zeros_like(ytile)
    barrier = pltpu.get_barrier_semaphore()
    for axis, index, there in sides:

        @pl.when(there)
        def _(axis=axis, index=index):
            pl.semaphore_signal(barrier, inc=1, device_id={axis: index}, device_id_type=MESH)

    pl.semaphore_wait(barrier, sum(there.astype(jnp.int32) for _, _, there in sides))

    def coef_copy(k):
        return pltpu.make_async_remote_copy(
            src_ref=coef, dst_ref=hc.at[k ^ 1], send_sem=csem.at[k], recv_sem=crsem.at[k ^ 1],
            device_id={sides[k][0]: sides[k][1]}, device_id_type=MESH,
        )

    def coef_arrival(k):
        return pltpu.make_async_remote_copy(
            src_ref=coef, dst_ref=hc.at[k], send_sem=csem.at[k], recv_sem=crsem.at[k],
            device_id={sides[k][0]: sides[k][1]}, device_id_type=MESH,
        )

    for k in range(4):

        @pl.when(sides[k][2])
        def _(k=k):
            coef_copy(k).start()

    def split(table, high, low, count, padded):
        value = table[...]
        high[...] = jnp.zeros_like(high)
        low[...] = jnp.zeros_like(low)
        top = value.astype(BF16)
        high[pl.ds(0, count), pl.ds(0, count)] = top
        low[pl.ds(0, count), pl.ds(0, count)] = (value - top.astype(F32)).astype(BF16)

    split(s5, sh5, sl5, Q5**3, sh5.shape[0])
    split(s3, sh3, sl3, Q3**3, sh3.shape[0])

    def spread_diagonal(table, inv, count):
        value = table[...]
        same = lax.broadcasted_iota(jnp.int32, value.shape, 0) == lax.broadcasted_iota(jnp.int32, value.shape, 1)
        column = jnp.sum(jnp.where(same, value, 0.0), axis=1, keepdims=True)
        wide = jnp.broadcast_to(column, (count, NZ))
        for y in range(NY):
            inv[pl.ds(y, count, stride=NY), :] = wide

    spread_diagonal(s5, inv5, Q5**3)
    spread_diagonal(s3, inv3, Q3**3)
    for n in range(Q1**3):
        inv1[pl.ds(n * NY, NY), :] = jnp.full((NY, NZ), s1[n, n])

    for k in range(4):

        @pl.when(sides[k][2])
        def _(k=k):
            coef_arrival(k).wait_recv()
            coef_copy(k).wait_send()

    row = lax.broadcasted_iota(jnp.int32, (NY, NZ), 0)
    lane = lax.broadcasted_iota(jnp.int32, (NY, NZ), 1)
    c = coef[...]
    bottom = jnp.zeros((NY, NZ), F32)
    top = jnp.zeros((NY, NZ), F32)
    for y in range(NY):
        bottom = jnp.where(row == y, ends[0, y].astype(F32), bottom)
        top = jnp.where(row == y, ends[1, y].astype(F32), top)
    y_before = jnp.where(row == 0, pltpu.roll(hc[2], 1, 0), pltpu.roll(c, 1, 0))
    y_after = jnp.where(row == NY - 1, pltpu.roll(hc[3], NY - 1, 0), pltpu.roll(c, NY - 1, 0))
    weights[0] = 0.5 * (c + hc[0])
    weights[1] = 0.5 * (c + hc[1])
    weights[2] = 0.5 * (c + y_before)
    weights[3] = 0.5 * (c + y_after)
    weights[4] = jnp.where(lane == 0, bottom * c, 0.5 * (c + pltpu.roll(c, 1, 1)))
    weights[5] = jnp.where(lane == NZ - 1, top * c, 0.5 * (c + pltpu.roll(c, NZ - 1, 1)))

    def invert(q, inv):
        p = PENALTY[q]
        xl, xh, yl, yh, zl, zh = (p * weights[k] for k in range(6))

        def body(i, carry):
            at = pl.ds(pl.multiple_of(i * q * q * NY, NY), q * q * NY)
            wx = jnp.where(i == 0, xl, 0.0) + jnp.where(i == q - 1, xh, 0.0)
            base = tiles(inv[at, :], q, q) * c + wx
            base = ends_added(base, q, (jnp.broadcast_to(yl, (q, NY, NZ)), jnp.broadcast_to(yh, (q, NY, NZ))),
                              (jnp.broadcast_to(zl, (q, NY, NZ)), jnp.broadcast_to(zh, (q, NY, NZ))))
            inv[at, :] = (1.0 / base).reshape(q * q * NY, NZ)
            return carry

        lax.fori_loop(0, q, body, 0)

    def ends_added(base, q, y_pair, z_pair):
        first = base[0:1] + y_pair[0][None]
        last = base[q - 1 : q] + y_pair[1][None]
        base = jnp.concatenate([first, base[1 : q - 1], last] if q > 2 else [first, last], 0)
        first = base[:, 0:1] + z_pair[0][:, None]
        last = base[:, q - 1 : q] + z_pair[1][:, None]
        return jnp.concatenate([first, base[:, 1 : q - 1], last] if q > 2 else [first, last], 1)

    invert(Q5, inv5)
    invert(Q3, inv3)
    invert(Q1, inv1)

    def face_copy(k, q, d, slot, arriving):
        face = q * q * NY
        if k < 2:
            src = d.at[pl.ds(0 if k == 0 else (q**3) * NY - face, face), :]
            dst = hx.at[slot, k if arriving else k ^ 1, pl.ds(0, face), :]
        else:
            src = pack.at[k - 2, pl.ds(0, q * NY), :]
            dst = hy.at[slot, (k if arriving else k ^ 1) - 2, pl.ds(0, q * NY), :]
        return pltpu.make_async_remote_copy(
            src_ref=src, dst_ref=dst,
            send_sem=ssem.at[k, slot], recv_sem=rsem.at[k if arriving else k ^ 1, slot],
            device_id={sides[k][0]: sides[k][1]}, device_id_type=MESH,
        )

    def send_faces(q, d, slot):
        for k in range(2):

            @pl.when(sides[k][2])
            def _(k=k):
                face_copy(k, q, d, slot, False).start()

        for i in range(q):
            pack[0, pl.ds(i * NY, q), :] = d[pl.ds(i * q * q * NY, q, stride=NY), :]
            pack[1, pl.ds(i * NY, q), :] = d[pl.ds((i * q * q + q * (q - 1)) * NY + NY - 1, q, stride=NY), :]
        for k in range(2, 4):

            @pl.when(sides[k][2])
            def _(k=k):
                face_copy(k, q, d, slot, False).start()

    def take_faces(q, d, slot):
        for k in range(4):

            @pl.when(sides[k][2])
            def _(k=k):
                face_copy(k, q, d, slot, True).wait_recv()

        for k in range(4):

            @pl.when(sides[k][2])
            def _(k=k):
                face_copy(k, q, d, slot, False).wait_send()

        for i in range(q):
            ytile[0, pl.ds(i * q * NY, q, stride=NY), :] = hy[slot, 0, pl.ds(i * NY, q), :]
            ytile[1, pl.ds(i * q * NY + NY - 1, q, stride=NY), :] = hy[slot, 1, pl.ds(i * NY, q), :]

    def product_wide(q, d, t, high, low):
        count = q**3
        padded = high.shape[0]
        s_high, s_low = high[...], low[...]
        for y in range(0, NY, 2):
            pair = [d[pl.ds(y + h, count, stride=NY), :] for h in range(2)]
            v = jnp.concatenate(pair, 1)
            if padded > count:
                v = jnp.concatenate([v, jnp.zeros((padded - count, 2 * NZ), F32)], 0)
            v_high = v.astype(BF16)
            v_low = (v - v_high.astype(F32)).astype(BF16)
            out = jnp.dot(s_high, v_high, preferred_element_type=F32)
            out += jnp.dot(s_high, v_low, preferred_element_type=F32)
            out += jnp.dot(s_low, v_high, preferred_element_type=F32)
            for h in range(2):
                t[pl.ds(y + h, count, stride=NY), :] = out[:count, h * NZ : (h + 1) * NZ]

    def product_small(d, t):
        count = Q1**3
        parts = [d[pl.ds(n * NY, NY), :] for n in range(count)]
        for m in range(count):
            total = s1[m, 0] * parts[0]
            for n in range(1, count):
                total += s1[m, n] * parts[n]
            t[pl.ds(m * NY, NY), :] = total

    def apply(level, slot):
        q, d, t, r = level["q"], level["d"], level["t"], level["r"]
        p = PENALTY[q]
        send_faces(q, d, slot)
        level["product"]()

        def local(i, carry):
            yl, yh, zl, zh = (p * weights[k] for k in range(2, 6))
            at = pl.ds(pl.multiple_of(i * q * q * NY, NY), q * q * NY)
            dv = tiles(d[at, :], q, q)
            lo, hi = dv[0], dv[q - 1]
            y_pair = (
                yl * (lo - jnp.where(row == 0, 0.0, pltpu.roll(hi, 1, 1))),
                yh * (hi - jnp.where(row == NY - 1, 0.0, pltpu.roll(lo, NY - 1, 1))),
            )
            lo, hi = dv[:, 0], dv[:, q - 1]
            z_pair = (
                zl * (lo - jnp.where(lane == 0, 0.0, pltpu.roll(hi, 1, 2))),
                zh * (hi - jnp.where(lane == NZ - 1, 0.0, pltpu.roll(lo, NZ - 1, 2))),
            )
            total = ends_added(tiles(t[at, :], q, q) * c, q, y_pair, z_pair)
            r[at, :] = r[at, :] - total.reshape(q * q * NY, NZ)
            return carry

        lax.fori_loop(0, q, local, 0)
        take_faces(q, d, slot)
        face = q * q * NY
        for k in range(2):
            at = pl.ds(0 if k == 0 else (q**3) * NY - face, face)
            step = p * weights[k] * tiles(d[at, :] - hx[slot, k, pl.ds(0, face), :], q * q)
            r[at, :] = r[at, :] - step.reshape(face, NZ)

        def rim(i, carry):
            for k in range(2):
                at = pl.ds(pl.multiple_of((i * q * q + k * q * (q - 1)) * NY, NY), q * NY)
                step = p * weights[2 + k] * tiles(ytile[k, pl.ds(pl.multiple_of(i * q * NY, NY), q * NY), :], q)
                r[at, :] = r[at, :] + step.reshape(q * NY, NZ)
            return carry

        lax.fori_loop(0, q, rim, 0)

    def first_update(level, factor, fresh):
        q, d, x, r, inv = level["q"], level["d"], level["x"], level["r"], level["inv"]

        def body(i, carry):
            at = pl.ds(pl.multiple_of(i * q * q * NY, NY), q * q * NY)
            step = inv[at, :] * r[at, :] * factor
            d[at, :] = step
            x[at, :] = step if fresh else x[at, :] + step
            return carry

        lax.fori_loop(0, q, body, 0)

    def next_update(level, a, b):
        q, d, x, r, inv = level["q"], level["d"], level["x"], level["r"], level["inv"]

        def body(i, carry):
            at = pl.ds(pl.multiple_of(i * q * q * NY, NY), q * q * NY)
            step = a * d[at, :] + b * inv[at, :] * r[at, :]
            d[at, :] = step
            x[at, :] = x[at, :] + step
            return carry

        lax.fori_loop(0, q, body, 0)

    def pick(k, values):
        out = jnp.float32(values[0])
        for n in range(1, len(values)):
            out = jnp.where(k == n, jnp.float32(values[n]), out)
        return out

    def smooth(level, steps, lowest, fresh, exchange, last):
        factor, pairs = chebyshev_factors(steps, lowest)
        first_update(level, factor, fresh)

        def body(k, carry):
            apply(level, lax.rem(exchange + k, 2))
            next_update(level, pick(k, [a for a, _ in pairs]), pick(k, [b for _, b in pairs]))
            return carry

        lax.fori_loop(0, steps - 1, body, 0)
        if last:
            apply(level, (exchange + steps - 1) % 2)

    def restrict(fine, coarse, qf, qc):
        table = lagrange(qf, qc)

        def body(j, carry):
            rows = [tiles(fine[pl.ds(pl.multiple_of((i * qf * qf + j * qf) * NY, NY), qf * NY), :], qf) for i in range(qf)]
            for a in range(qc):
                along = weighted(table[:, a], rows)
                out = [weighted(table[:, e], [along[k] for k in range(qf)]) for e in range(qc)]
                for e in range(qc):
                    work[pl.ds(pl.multiple_of((j * qc * qc + a * qc + e) * NY, NY), NY), :] = out[e]
            return carry

        lax.fori_loop(0, qf, body, 0)

        def gather(a, carry):
            rows = [work[pl.ds(pl.multiple_of((j * qc * qc + a * qc) * NY, NY), qc * NY), :] for j in range(qf)]
            for b in range(qc):
                coarse[pl.ds(pl.multiple_of((a * qc * qc + b * qc) * NY, NY), qc * NY), :] = weighted(table[:, b], rows)
            return carry

        lax.fori_loop(0, qc, gather, 0)

    def prolong(coarse, fine, sum_into, qf, qc):
        table = lagrange(qf, qc)

        def spread(a, carry):
            rows = [coarse[pl.ds(pl.multiple_of((a * qc * qc + b * qc) * NY, NY), qc * NY), :] for b in range(qc)]
            for j in range(qf):
                work[pl.ds(pl.multiple_of((j * qc * qc + a * qc) * NY, NY), qc * NY), :] = weighted(table[j], rows)
            return carry

        lax.fori_loop(0, qc, spread, 0)

        def body(j, carry):
            along = []
            for a in range(qc):
                part = tiles(work[pl.ds(pl.multiple_of((j * qc * qc + a * qc) * NY, NY), qc * NY), :], qc)
                along.append([weighted(table[k], [part[e] for e in range(qc)]) for k in range(qf)])
            for i in range(qf):
                for k in range(qf):
                    value = weighted(table[i], [along[a][k] for a in range(qc)])
                    at = pl.ds(pl.multiple_of((i * qf * qf + j * qf + k) * NY, NY), NY)
                    fine[at, :] = value
                    sum_into[at, :] = sum_into[at, :] + value
            return carry

        lax.fori_loop(0, qf, body, 0)

    five = dict(q=Q5, d=d5, t=t5, r=res, x=sol, inv=inv5, product=lambda: product_wide(Q5, d5, t5, sh5, sl5))
    three = dict(q=Q3, d=d3, t=t3, r=r3, x=x3, inv=inv3, product=lambda: product_wide(Q3, d3, t3, sh3, sl3))
    one = dict(q=Q1, d=d1, t=t1, r=r1, x=x1, inv=inv1, product=lambda: product_small(d1, t1))

    res[...] = rhs[...]
    smooth(five, DEGREE, LAMBDA_TOP / 8.0, True, 0, True)
    restrict(res, r3, Q5, Q3)
    smooth(three, DEGREE, LAMBDA_TOP / 8.0, True, 3, True)
    restrict(r3, r1, Q3, Q1)
    smooth(one, COARSE_ITERS, LAMBDA_TOP / 40.0, True, 6, False)
    prolong(x1, d3, x3, Q3, Q1)
    apply(three, 13 % 2)
    smooth(three, DEGREE, LAMBDA_TOP / 8.0, False, 14, False)
    prolong(x3, d5, sol, Q5, Q3)
    apply(five, 16 % 2)
    smooth(five, DEGREE, LAMBDA_TOP / 8.0, False, 17, True)


def per_device(right_side, coefficient, bottom_top, stiff_five, stiff_three, stiff_one):
    shape = right_side.shape
    n5, n3, n1 = Q5**3 * NY, Q3**3 * NY, Q1**3 * NY
    vmem = pl.BlockSpec(memory_space=pltpu.VMEM)
    smem = pl.BlockSpec(memory_space=pltpu.SMEM)
    field = lambda n: pltpu.VMEM((n, NZ), F32)
    dma = pltpu.SemaphoreType.DMA
    sol, res = pl.pallas_call(
        kernel,
        out_shape=[jax.ShapeDtypeStruct((n5, NZ), F32)] * 2,
        in_specs=[vmem, smem, vmem, vmem, vmem, smem],
        out_specs=[vmem, vmem],
        scratch_shapes=[
            field(n5), field(n5), field(n5),
            field(n3), field(n3), field(n3), field(n3), field(n3),
            field(n1), field(n1), field(n1), field(n1), field(n1),
            pltpu.VMEM((224, 224), BF16), pltpu.VMEM((224, 224), BF16),
            pltpu.VMEM((64, 64), BF16), pltpu.VMEM((64, 64), BF16),
            field(6 * 16 * NY), pltpu.VMEM((6, NY, NZ), F32),
            pltpu.VMEM((2, 2, Q5 * Q5 * NY, NZ), F32), pltpu.VMEM((2, 2, Q5 * NY, NZ), F32),
            pltpu.VMEM((2, Q5 * Q5 * NY, NZ), F32), pltpu.VMEM((2, Q5 * NY, NZ), F32), pltpu.VMEM((4, NY, NZ), F32),
            dma((4, 2)), dma((4, 2)), dma((4,)), dma((4,)),
        ],
        compiler_params=pltpu.CompilerParams(
            collective_id=0, has_side_effects=True, vmem_limit_bytes=48 * 2**20
        ),
    )(
        coefficient.reshape(NY, NZ), bottom_top.reshape(2, NY), right_side.reshape(n5, NZ),
        stiff_five, stiff_three, stiff_one,
    )
    return sol.reshape(shape), res.reshape(shape)


def solution(mesh):
    field = P(None, None, None, "slab", "cross", None)
    return jax.shard_map(
        per_device,
        mesh=mesh,
        in_specs=(field, P("slab", "cross", None), P(None, "slab", "cross"), P(), P(), P()),
        out_specs=(field, field),
        check_vma=False,
    )
```

profile of v0, /device:TPU:13, one launch (start us, length us, event | category | flops | bytes accessed | tf_op | source)
XLA Modules:
  0.0 124.0 jit_solution(179807953520082448)
XLA Ops:
  0.6 0.0 copy-start.3
  0.6 0.0 copy-start.5
  0.7 0.7 copy-done.3
  1.3 0.0 copy-done.5
  1.3 0.0 copy-start
  1.3 1.2 copy-done
  2.5 0.0 copy-start.1
  2.5 0.9 copy-done.1
  3.4 0.0 copy-start.2
  3.4 0.8 copy-done.2
  4.2 0.0 copy-start.4
  4.2 0.7 copy-done.4
  4.9 117.3 %shard_map.77 = (f32[1728,128]{1,0:T(8,128)S(1)}, f32[1728,128]{1,0:T(8,128)S(1)}) custom-call(f32[8,128]{1,0:T(8,128)S(1)} %bitcast.12, s32[2,8]{1,0:T(2,128)S(1)} %bitcast.13, f32[1728,128]{1,0:T(8,128)S(1)} %bitcast.11, f32[216,216]{1,0:T(8,128)S(1)} %copy-done.1, f32[64,64]{1,0:T(8,128)S(1)} %copy-done.2, f32[8,8]{1,0:T(8,128)S(1)} %copy-done.4), custom_call_target="tpu_custom_call" | custom-call | tf_op jit(solution)/shard_map/pallas_call | solution.py:410
  122.1 0.9 copy.12
  123.1 0.9 copy.13
Async XLA Ops:
  0.6 0.7 copy-start.3
  0.6 0.7 copy-start.5
  1.3 1.2 copy-start
  2.5 0.9 copy-start.1
  3.4 0.8 copy-start.2
  4.2 0.7 copy-start.4
where the time goes:
time: 124 us
  Pallas kernels  117 us (94%)
  local copies, waits for them, and re-layouts  6.05 us (5%)
    pallas_call x1, Pallas kernels, per_device(): pl.pallas_call(kernel, out_shape=[jax.ShapeDtypeStruct((n5, NZ), F32)] *...  117 us
    unnamed x14, local copies, waits for them, and re-layouts  6.05 us

commit v1 on v0

v1 whole, which is shorter than its diff:
```python
import functools

import jax
import jax.numpy as jnp
import numpy as np
from jax import lax
from jax.experimental import pallas as pl
from jax.experimental.pallas import tpu as pltpu
from jax.sharding import PartitionSpec as P

MESH = pl.DeviceIdType.MESH
F32 = jnp.float32
BF16 = jnp.bfloat16
Q5, Q3, Q1 = 6, 4, 2
DEGREE = 3
COARSE_ITERS = 8
LAMBDA_TOP = 2.2
NY, NZ = 8, 128
PENALTY = {Q5: 3.0, Q3: 2.0, Q1: 1.0}


def lagrange(fine_count, coarse_count):
    fine = np.linspace(-1.0, 1.0, fine_count)
    coarse = np.linspace(-1.0, 1.0, coarse_count)
    table = np.ones((fine_count, coarse_count))
    for c in range(coarse_count):
        for o in range(coarse_count):
            if o != c:
                table[:, c] = table[:, c] * (fine - coarse[o]) / (coarse[c] - coarse[o])
    return table.astype(np.float32)


def chebyshev_factors(steps, lowest):
    center = 0.5 * (LAMBDA_TOP + lowest)
    radius = 0.5 * (LAMBDA_TOP - lowest)
    sigma = center / radius
    rho = 1.0 / sigma
    pairs = []
    for _ in range(steps - 1):
        rho_next = 1.0 / (2.0 * sigma - rho)
        pairs.append((rho_next * rho, 2.0 * rho_next / radius))
        rho = rho_next
    return 1.0 / center, pairs


def weighted(table_row, terms):
    total = None
    for value, term in zip(table_row, terms):
        if value == 0.0:
            continue
        part = term if value == 1.0 else float(value) * term
        total = part if total is None else total + part
    return total


def tiles(value, *lead):
    return value.reshape(*lead, NY, NZ)


def kernel(
    coef_in, ends_in, rhs_in, s5_in, s3_in, s1_in, sol, res,
    coef, ends, s5, s3, s1,
    d5, t5, inv5, x3, r3, d3, t3, inv3, x1, r1, d1, t1, inv1,
    sh5, sl5, sh3, sl3, work, weights, hx, hy, ytile, pack, hc,
    xs, xr, ys, yr, csem, crsem, load,
):
    slab, cross = lax.axis_index("slab"), lax.axis_index("cross")
    ns, nc = lax.axis_size("slab"), lax.axis_size("cross")
    sides = (
        ("slab", slab - 1, slab > 0),
        ("slab", slab + 1, slab < ns - 1),
        ("cross", cross - 1, cross > 0),
        ("cross", cross + 1, cross < nc - 1),
    )
    hc[...] = jnp.zeros_like(hc)
    hx[...] = jnp.zeros_like(hx)
    hy[...] = jnp.zeros_like(hy)
    ytile[...] = jnp.zeros_like(ytile)
    barrier = pltpu.get_barrier_semaphore()
    for axis, index, there in sides:

        @pl.when(there)
        def _(axis=axis, index=index):
            pl.semaphore_signal(barrier, inc=1, device_id={axis: index}, device_id_type=MESH)

    pairs = ((coef_in, coef), (s5_in, s5), (s3_in, s3), (rhs_in, res), (ends_in, ends), (s1_in, s1))
    loads = [pltpu.make_async_copy(src, dst, load.at[n]) for n, (src, dst) in enumerate(pairs)]
    for copy in loads:
        copy.start()
    loads[0].wait()
    pl.semaphore_wait(barrier, sum(there.astype(jnp.int32) for _, _, there in sides))

    def coef_copy(k, arriving):
        here = k if arriving else k ^ 1
        return pltpu.make_async_remote_copy(
            src_ref=coef, dst_ref=hc.at[here], send_sem=csem.at[k], recv_sem=crsem.at[here],
            device_id={sides[k][0]: sides[k][1]}, device_id_type=MESH,
        )

    for k in range(4):

        @pl.when(sides[k][2])
        def _(k=k):
            coef_copy(k, False).start()

    for copy in loads[1:]:
        copy.wait()

    def split(table, high, low, count):
        value = table[...]
        high[...] = jnp.zeros_like(high)
        low[...] = jnp.zeros_like(low)
        top = value.astype(BF16)
        high[pl.ds(0, count), pl.ds(0, count)] = top
        low[pl.ds(0, count), pl.ds(0, count)] = (value - top.astype(F32)).astype(BF16)

    split(s5, sh5, sl5, Q5**3)
    split(s3, sh3, sl3, Q3**3)

    def spread_diagonal(table, inv, count):
        value = table[...]
        same = lax.broadcasted_iota(jnp.int32, value.shape, 0) == lax.broadcasted_iota(jnp.int32, value.shape, 1)
        column = jnp.sum(jnp.where(same, value, 0.0), axis=1, keepdims=True)
        wide = jnp.broadcast_to(column, (count, NZ))
        for y in range(NY):
            inv[pl.ds(y, count, stride=NY), :] = wide

    spread_diagonal(s5, inv5, Q5**3)
    spread_diagonal(s3, inv3, Q3**3)
    for n in range(Q1**3):
        inv1[pl.ds(n * NY, NY), :] = jnp.full((NY, NZ), s1[n, n])

    for k in range(4):

        @pl.when(sides[k][2])
        def _(k=k):
            coef_copy(k, True).wait_recv()
            coef_copy(k, False).wait_send()

    row = lax.broadcasted_iota(jnp.int32, (NY, NZ), 0)
    lane = lax.broadcasted_iota(jnp.int32, (NY, NZ), 1)
    c = coef[...]
    bottom = jnp.zeros((NY, NZ), F32)
    top = jnp.zeros((NY, NZ), F32)
    for y in range(NY):
        bottom = jnp.where(row == y, ends[0, y].astype(F32), bottom)
        top = jnp.where(row == y, ends[1, y].astype(F32), top)
    y_before = jnp.where(row == 0, pltpu.roll(hc[2], 1, 0), pltpu.roll(c, 1, 0))
    y_after = jnp.where(row == NY - 1, pltpu.roll(hc[3], NY - 1, 0), pltpu.roll(c, NY - 1, 0))
    weights[0] = 0.5 * (c + hc[0])
    weights[1] = 0.5 * (c + hc[1])
    weights[2] = 0.5 * (c + y_before)
    weights[3] = 0.5 * (c + y_after)
    weights[4] = jnp.where(lane == 0, bottom * c, 0.5 * (c + pltpu.roll(c, 1, 1)))
    weights[5] = jnp.where(lane == NZ - 1, top * c, 0.5 * (c + pltpu.roll(c, NZ - 1, 1)))

    def ends_added(base, q, y_pair, z_pair):
        first = base[0:1] + y_pair[0][None]
        last = base[q - 1 : q] + y_pair[1][None]
        base = jnp.concatenate([first, base[1 : q - 1], last] if q > 2 else [first, last], 0)
        first = base[:, 0:1] + z_pair[0][:, None]
        last = base[:, q - 1 : q] + z_pair[1][:, None]
        return jnp.concatenate([first, base[:, 1 : q - 1], last] if q > 2 else [first, last], 1)

    def slab_weight(i, q):
        return jnp.where(i == 0, PENALTY[q] * weights[0], 0.0) + jnp.where(i == q - 1, PENALTY[q] * weights[1], 0.0)

    def plane_at(i, q):
        return pl.ds(pl.multiple_of(i * (q * q * NY), NY), q * q * NY)

    def invert(q, inv):
        yl, yh, zl, zh = (jnp.broadcast_to(PENALTY[q] * weights[k], (q, NY, NZ)) for k in range(2, 6))

        def body(i, carry):
            at = plane_at(i, q)
            base = tiles(inv[at, :], q, q) * c + slab_weight(i, q)
            base = ends_added(base, q, (yl, yh), (zl, zh))
            inv[at, :] = (1.0 / base).reshape(q * q * NY, NZ)
            return carry

        lax.fori_loop(0, q, body, 0)

    invert(Q5, inv5)
    invert(Q3, inv3)
    invert(Q1, inv1)

    def lines(q):
        return [(0, 1), (q - 1, 1)] + [(j, min(2, q - 1 - j)) for j in range(1, q - 1, 2)]

    def slab_copy(k, q, d, slot, piece, arriving):
        first, count = lines(q)[piece]
        size = count * q * NY
        base = 0 if k == 0 else (q**3 - q * q) * NY
        here = k if arriving else k ^ 1
        return pltpu.make_async_remote_copy(
            src_ref=d.at[slot, pl.ds(base + first * q * NY, size), :],
            dst_ref=hx.at[slot, here, pl.ds(first * q * NY, size), :],
            send_sem=xs.at[k, piece, slot], recv_sem=xr.at[here, piece, slot],
            device_id={"slab": sides[k][1]}, device_id_type=MESH,
        )

    def cross_copy(k, q, slot, arriving):
        here = k if arriving else k ^ 1
        return pltpu.make_async_remote_copy(
            src_ref=pack.at[slot, k, pl.ds(0, q * NY), :], dst_ref=hy.at[slot, here, pl.ds(0, q * NY), :],
            send_sem=ys.at[k, slot], recv_sem=yr.at[here, slot],
            device_id={"cross": sides[2 + k][1]}, device_id_type=MESH,
        )

    def slab_do(k, method, *args):
        @pl.when(sides[k][2])
        def _():
            getattr(slab_copy(k, *args), method)()

    def cross_do(k, method, *args):
        @pl.when(sides[2 + k][2])
        def _():
            getattr(cross_copy(k, *args), method)()

    def send_slab(q, d, slot, pieces):
        for piece in pieces:
            for k in range(2):
                slab_do(k, "start", q, d, slot, piece, False)

    def send_cross(q, d, slot):
        for i in range(q):
            pack[slot, 0, pl.ds(i * NY, q), :] = d[slot, pl.ds(i * q * q * NY, q, stride=NY), :]
            pack[slot, 1, pl.ds(i * NY, q), :] = d[slot, pl.ds((i * q * q + q * (q - 1)) * NY + NY - 1, q, stride=NY), :]
        for k in range(2):
            cross_do(k, "start", q, slot, False)

    def send_all(q, d, slot):
        send_cross(q, d, slot)
        send_slab(q, d, slot, range(len(lines(q))))

    def product_wide(q, d, slot, t, high, low):
        count = q**3
        padded = high.shape[0]
        s_high, s_low = high[...], low[...]
        for y in range(0, NY, 2):
            pair = [d[slot, pl.ds(y + h, count, stride=NY), :] for h in range(2)]
            v = jnp.concatenate(pair, 1)
            if padded > count:
                v = jnp.concatenate([v, jnp.zeros((padded - count, 2 * NZ), F32)], 0)
            v_high = v.astype(BF16)
            v_low = (v - v_high.astype(F32)).astype(BF16)
            out = jnp.dot(s_high, v_high, preferred_element_type=F32)
            out += jnp.dot(s_high, v_low, preferred_element_type=F32)
            out += jnp.dot(s_low, v_high, preferred_element_type=F32)
            for h in range(2):
                t[pl.ds(y + h, count, stride=NY), :] = out[:count, h * NZ : (h + 1) * NZ]

    def product_small(d, slot, t):
        count = Q1**3
        parts = [d[slot, pl.ds(n * NY, NY), :] for n in range(count)]
        for m in range(count):
            total = s1[m, 0] * parts[0]
            for n in range(1, count):
                total += s1[m, n] * parts[n]
            t[pl.ds(m * NY, NY), :] = total

    def step(level, slot, a, b, update, send):
        q, d, t, r, x, inv = (level[name] for name in ("q", "d", "t", "r", "x", "inv"))
        p = PENALTY[q]
        other = 1 - slot
        level["product"](slot)

        def local(i, carry):
            yl, yh, zl, zh = (p * weights[k] for k in range(2, 6))
            at = plane_at(i, q)
            dv = tiles(d[slot, at, :], q, q)
            lo, hi = dv[0], dv[q - 1]
            y_pair = (
                yl * (lo - jnp.where(row == 0, 0.0, pltpu.roll(hi, 1, 1))),
                yh * (hi - jnp.where(row == NY - 1, 0.0, pltpu.roll(lo, NY - 1, 1))),
            )
            lo, hi = dv[:, 0], dv[:, q - 1]
            z_pair = (
                zl * (lo - jnp.where(lane == 0, 0.0, pltpu.roll(hi, 1, 2))),
                zh * (hi - jnp.where(lane == NZ - 1, 0.0, pltpu.roll(lo, NZ - 1, 2))),
            )
            total = ends_added(tiles(t[at, :], q, q) * c, q, y_pair, z_pair)
            r[at, :] = r[at, :] - total.reshape(q * q * NY, NZ)
            return carry

        lax.fori_loop(0, q, local, 0)
        face = q * q * NY
        for k in range(2):
            at = pl.ds(0 if k == 0 else (q**3) * NY - face, face)
            r[at, :] = r[at, :] - (p * weights[k] * tiles(d[slot, at, :], q * q)).reshape(face, NZ)

        for k in range(2):
            cross_do(k, "wait_recv", q, slot, True)
        for i in range(q):
            ytile[0, pl.ds(i * q * NY, q, stride=NY), :] = hy[slot, 0, pl.ds(i * NY, q), :]
            ytile[1, pl.ds(i * q * NY + NY - 1, q, stride=NY), :] = hy[slot, 1, pl.ds(i * NY, q), :]

        def rim(i, carry):
            for k in range(2):
                at = pl.ds(pl.multiple_of(i * (q * q * NY) + k * q * (q - 1) * NY, NY), q * NY)
                part = p * weights[2 + k] * tiles(ytile[k, pl.ds(pl.multiple_of(i * (q * NY), NY), q * NY), :], q)
                r[at, :] = r[at, :] + part.reshape(q * NY, NZ)
            return carry

        lax.fori_loop(0, q, rim, 0)

        def advance(at):
            value = a * d[slot, at, :] + b * inv[at, :] * r[at, :]
            d[other, at, :] = value
            x[at, :] = x[at, :] + value

        if update and q > 2:

            def inside(i, carry):
                advance(plane_at(i, q))
                return carry

            lax.fori_loop(1, q - 1, inside, 0)

        pieces = lines(q)
        groups = [[0, 1]] + [[n] for n in range(2, len(pieces))]
        for number, group in enumerate(groups):
            for piece in group:
                first, count = pieces[piece]
                size = count * q * NY
                for k in range(2):
                    slab_do(k, "wait_recv", q, d, slot, piece, True)
                    at = pl.ds((0 if k == 0 else (q**3 - q * q) * NY) + first * q * NY, size)
                    part = p * weights[k] * tiles(hx[slot, k, pl.ds(first * q * NY, size), :], count * q)
                    r[at, :] = r[at, :] + part.reshape(size, NZ)
                    if update:
                        advance(at)
            if send:
                if number == 0:
                    send_cross(q, d, other)
                send_slab(q, d, other, group)
        for k in range(2):
            cross_do(k, "wait_send", q, slot, False)
            for piece in range(len(pieces)):
                slab_do(k, "wait_send", q, d, slot, piece, False)

    def first_update(level, slot, factor):
        q, d, x, r, inv = (level[name] for name in ("q", "d", "x", "r", "inv"))

        def body(i, carry):
            at = plane_at(i, q)
            value = inv[at, :] * r[at, :] * factor
            d[slot, at, :] = value
            x[at, :] = value
            return carry

        lax.fori_loop(0, q, body, 0)
        send_all(q, d, slot)

    def pick(k, values):
        out = jnp.float32(values[0])
        for n in range(1, len(values)):
            out = jnp.where(k == n, jnp.float32(values[n]), out)
        return out

    def run(level, exchange, factors, last):
        loop = len(factors) if last else len(factors) - 1

        def body(k, carry):
            a, b = pick(k, [f[0] for f in factors]), pick(k, [f[1] for f in factors])
            step(level, lax.rem(exchange + k, 2), a, b, True, True)
            return carry

        lax.fori_loop(0, loop, body, 0)
        slot = (exchange + loop) % 2
        if last:
            step(level, slot, 0.0, 0.0, False, False)
        else:
            step(level, slot, *factors[-1], True, False)

    def restrict(fine, coarse, qf, qc):
        table = lagrange(qf, qc)

        def body(j, carry):
            rows = [tiles(fine[pl.ds(pl.multiple_of(j * (qf * NY) + i * qf * qf * NY, NY), qf * NY), :], qf) for i in range(qf)]
            for a in range(qc):
                along = weighted(table[:, a], rows)
                for e in range(qc):
                    out = weighted(table[:, e], [along[k] for k in range(qf)])
                    work[pl.ds(pl.multiple_of(j * (qc * qc * NY) + (a * qc + e) * NY, NY), NY), :] = out
            return carry

        lax.fori_loop(0, qf, body, 0)

        def gather(a, carry):
            rows = [work[pl.ds(pl.multiple_of(a * (qc * NY) + j * qc * qc * NY, NY), qc * NY), :] for j in range(qf)]
            for b in range(qc):
                at = pl.ds(pl.multiple_of(a * (qc * qc * NY) + b * qc * NY, NY), qc * NY)
                coarse[at, :] = weighted(table[:, b], rows)
            return carry

        lax.fori_loop(0, qc, gather, 0)

    def prolong(coarse, fine, slot, sum_into, qf, qc):
        table = lagrange(qf, qc)

        def spread(a, carry):
            rows = [coarse[pl.ds(pl.multiple_of(a * (qc * qc * NY) + b * qc * NY, NY), qc * NY), :] for b in range(qc)]
            for j in range(qf):
                at = pl.ds(pl.multiple_of(a * (qc * NY) + j * qc * qc * NY, NY), qc * NY)
                work[at, :] = weighted(table[j], rows)
            return carry

        lax.fori_loop(0, qc, spread, 0)

        def body(j, carry):
            along = []
            for a in range(qc):
                at = pl.ds(pl.multiple_of(j * (qc * qc * NY) + a * qc * NY, NY), qc * NY)
                part = tiles(work[at, :], qc)
                along.append([weighted(table[k], [part[e] for e in range(qc)]) for k in range(qf)])
            for i in range(qf):
                for k in range(qf):
                    value = weighted(table[i], [along[a][k] for a in range(qc)])
                    at = pl.ds(pl.multiple_of(j * (qf * NY) + (i * qf * qf + k) * NY, NY), NY)
                    fine[slot, at, :] = value
                    sum_into[at, :] = sum_into[at, :] + value
            return carry

        lax.fori_loop(0, qf, body, 0)
        send_all(qf, fine, slot)

    five = dict(q=Q5, d=d5, t=t5, r=res, x=sol, inv=inv5, product=lambda slot: product_wide(Q5, d5, slot, t5, sh5, sl5))
    three = dict(q=Q3, d=d3, t=t3, r=r3, x=x3, inv=inv3, product=lambda slot: product_wide(Q3, d3, slot, t3, sh3, sl3))
    one = dict(q=Q1, d=d1, t=t1, r=r1, x=x1, inv=inv1, product=lambda slot: product_small(d1, slot, t1))

    first, pairs = chebyshev_factors(DEGREE, LAMBDA_TOP / 8.0)
    coarse_first, coarse_pairs = chebyshev_factors(COARSE_ITERS, LAMBDA_TOP / 40.0)
    first_update(five, 0, first)
    run(five, 0, pairs, True)
    restrict(res, r3, Q5, Q3)
    first_update(three, 1, first)
    run(three, 3, pairs, True)
    restrict(r3, r1, Q3, Q1)
    first_update(one, 0, coarse_first)
    run(one, 6, coarse_pairs, False)
    prolong(x1, d3, 1, x3, Q3, Q1)
    run(three, 13, [(0.0, first)] + pairs, False)
    prolong(x3, d5, 0, sol, Q5, Q3)
    run(five, 16, [(0.0, first)] + pairs, True)


def per_device(right_side, coefficient, bottom_top, stiff_five, stiff_three, stiff_one):
    shape = right_side.shape
    n5, n3, n1 = Q5**3 * NY, Q3**3 * NY, Q1**3 * NY
    vmem = pl.BlockSpec(memory_space=pltpu.VMEM)
    hbm = pl.BlockSpec(memory_space=pltpu.HBM)
    field = lambda n: pltpu.VMEM((n, NZ), F32)
    pair = lambda n: pltpu.VMEM((2, n, NZ), F32)
    dma = pltpu.SemaphoreType.DMA
    sol, res = pl.pallas_call(
        kernel,
        out_shape=[jax.ShapeDtypeStruct((n5, NZ), F32)] * 2,
        in_specs=[hbm] * 6,
        out_specs=[vmem, vmem],
        scratch_shapes=[
            field(NY), pltpu.SMEM((2, NY), jnp.int32), pltpu.VMEM((Q5**3, Q5**3), F32), pltpu.VMEM((Q3**3, Q3**3), F32),
            pltpu.SMEM((Q1**3, Q1**3), F32),
            pair(n5), field(n5), field(n5),
            field(n3), field(n3), pair(n3), field(n3), field(n3),
            field(n1), field(n1), pair(n1), field(n1), field(n1),
            pltpu.VMEM((224, 224), BF16), pltpu.VMEM((224, 224), BF16),
            pltpu.VMEM((64, 64), BF16), pltpu.VMEM((64, 64), BF16),
            field(6 * 16 * NY), pltpu.VMEM((6, NY, NZ), F32),
            pltpu.VMEM((2, 2, Q5 * Q5 * NY, NZ), F32), pltpu.VMEM((2, 2, Q5 * NY, NZ), F32),
            pltpu.VMEM((2, Q5 * Q5 * NY, NZ), F32), pltpu.VMEM((2, 2, Q5 * NY, NZ), F32), pltpu.VMEM((4, NY, NZ), F32),
            dma((2, 4, 2)), dma((2, 4, 2)), dma((2, 2)), dma((2, 2)), dma((4,)), dma((4,)), dma((6,)),
        ],
        compiler_params=pltpu.CompilerParams(
            collective_id=0, has_side_effects=True, vmem_limit_bytes=48 * 2**20
        ),
    )(
        coefficient.reshape(NY, NZ), bottom_top.reshape(2, NY), right_side.reshape(n5, NZ),
        stiff_five, stiff_three, stiff_one,
    )
    return sol.reshape(shape), res.reshape(shape)


def solution(mesh):
    field = P(None, None, None, "slab", "cross", None)
    return jax.shard_map(
        per_device,
        mesh=mesh,
        in_specs=(field, P("slab", "cross", None), P(None, "slab", "cross"), P(), P(), P()),
        out_specs=(field, field),
        check_vma=False,
    )
```

time: 124 us -> 104 us (0.84); the launches traced: 124 us -> 102 us
  Pallas kernels: 117 us -> 95.4 us
    pallas_call x1, Pallas kernels: 117 us -> 95.4 us  [per_device(): pl.pallas_call(kernel, out_shape=[jax.ShapeDtypeStruct((n5, NZ), F32)] *...]
where the time goes in v1:
time: 104 us; the launch traced here: 102 us
  Pallas kernels  95.4 us (92%)
  local copies, waits for them, and re-layouts  6.05 us (6%)
    pallas_call x1, Pallas kernels, per_device(): pl.pallas_call(kernel, out_shape=[jax.ShapeDtypeStruct((n5, NZ), F32)] *...  95.4 us
    unnamed x14, local copies, waits for them, and re-layouts  6.05 us

profile of v1, /device:TPU:13, one launch (start us, length us, event | category | flops | bytes accessed | tf_op | source)
XLA Modules:
  0.0 102.1 jit_solution(13970907631275648823)
XLA Ops:
  0.6 0.0 copy-start.3
  0.6 0.0 copy-start.5
  0.7 0.7 copy-done.3
  1.3 0.0 copy-done.5
  1.3 0.0 copy-start
  1.3 1.2 %copy-done = f32[6,6,6,1,8,128]{5,4,3,2,1,0:T(8,128)S(1)} copy-done((f32[6,6,6,1,8,128]{5,4,3,2,1,0:T(8,128)S(1)}, f32[6,6,6,1,8,128]{5,4,3,2,1,0:T(8,128)}, u32[]{:S(2)}) %copy-start) | copy-done | bytes 884760
  2.5 0.0 copy-start.1
  2.5 0.9 copy-done.1
  3.4 0.0 copy-start.2
  3.4 0.8 copy-done.2
  4.2 0.0 copy-start.4
  4.2 0.7 copy-done.4
  4.9 95.4 %shard_map.77 = (f32[1728,128]{1,0:T(8,128)S(1)}, f32[1728,128]{1,0:T(8,128)S(1)}) custom-call(f32[8,128]{1,0:T(8,128)S(1)} %bitcast.12, s32[2,8]{1,0:T(2,128)S(1)} %bitcast.13, f32[1728,128]{1,0:T(8,128)S(1)} %bitcast.11, f32[216,216]{1,0:T(8,128)S(1)} %copy-done.1, f32[64,64]{1,0:T(8,128)S(1)} %copy-done.2, f32[8,8]{1,0:T(8,128)S(1)} %copy-done.4), custom_call_target="tpu_custom_call" | custom-call | tf_op jit(solution)/shard_map/pallas_call | solution.py:456
  100.2 0.9 copy.12
  101.2 0.9 copy.13
Async XLA Ops:
  0.6 0.7 copy-start.3
  0.6 0.7 copy-start.5
  1.3 1.2 %copy-start = (f32[6,6,6,1,8,128]{5,4,3,2,1,0:T(8,128)S(1)}, f32[6,6,6,1,8,128]{5,4,3,2,1,0:T(8,128)}, u32[]{:S(2)}) copy-start(f32[6,6,6,1,8,128]{5,4,3,2,1,0:T(8,128)} %param.6) | copy-start | bytes 2654212
  2.5 0.9 copy-start.1
  3.4 0.8 copy-start.2
  4.2 0.7 copy-start.4

commit v2 on v1

--- a/solution.py
+++ b/solution.py
@@ -16,6 +16,7 @@
 COARSE_ITERS = 8
 LAMBDA_TOP = 2.2
 NY, NZ = 8, 128
+SLOTS = 4
 PENALTY = {Q5: 3.0, Q3: 2.0, Q1: 1.0}
 
 
@@ -62,7 +63,8 @@
     coef, ends, s5, s3, s1,
     d5, t5, inv5, x3, r3, d3, t3, inv3, x1, r1, d1, t1, inv1,
     sh5, sl5, sh3, sl3, work, weights, hx, hy, ytile, pack, hc,
-    xs, xr, ys, yr, csem, crsem, load,
+    hd, dpack, dtile, gx3, gx1, gy3, gy1, gp3, gp1, gw,
+    xs, xr, ys, yr, cs, cr, gs, gr, csem, crsem, load,
 ):
     slab, cross = lax.axis_index("slab"), lax.axis_index("cross")
     ns, nc = lax.axis_size("slab"), lax.axis_size("cross")
@@ -72,23 +74,54 @@
         ("cross", cross - 1, cross > 0),
         ("cross", cross + 1, cross < nc - 1),
     )
-    hc[...] = jnp.zeros_like(hc)
-    hx[...] = jnp.zeros_like(hx)
-    hy[...] = jnp.zeros_like(hy)
-    ytile[...] = jnp.zeros_like(ytile)
+    corners = [
+        ({"slab": slab + 2 * k - 1, "cross": cross + 2 * m - 1}, sides[k][2] & sides[2 + m][2])
+        for k in range(2) for m in range(2)
+    ]
+
+    for k in range(2):
+
+        @pl.when(jnp.logical_not(sides[k][2]))
+        def _(k=k):
+            hc[k] = jnp.zeros_like(hc[k])
+            gw[k] = jnp.zeros_like(gw[k])
+            gx3[k] = jnp.zeros_like(gx3[k])
+            gx1[k] = jnp.zeros_like(gx1[k])
+            for slot in range(SLOTS):
+                hx[slot, k] = jnp.zeros_like(hx[slot, k])
+
+        @pl.when(jnp.logical_not(sides[2 + k][2]))
+        def _(k=k):
+            hc[2 + k] = jnp.zeros_like(hc[2 + k])
+            gw[2 + k] = jnp.zeros_like(gw[2 + k])
+            gy3[k] = jnp.zeros_like(gy3[k])
+            gy1[k] = jnp.zeros_like(gy1[k])
+            for slot in range(SLOTS):
+                hy[slot, k] = jnp.zeros_like(hy[slot, k])
+
+    for g in range(4):
+
+        @pl.when(jnp.logical_not(corners[g][1]))
+        def _(g=g):
+            for slot in range(SLOTS):
+                hd[slot, g] = jnp.zeros_like(hd[slot, g])
+
     barrier = pltpu.get_barrier_semaphore()
-    for axis, index, there in sides:
+    peers = [({axis: index}, there) for axis, index, there in sides] + corners
+    for device, there in peers:
 
         @pl.when(there)
-        def _(axis=axis, index=index):
-            pl.semaphore_signal(barrier, inc=1, device_id={axis: index}, device_id_type=MESH)
+        def _(device=device):
+            pl.semaphore_signal(barrier, inc=1, device_id=device, device_id_type=MESH)
 
     pairs = ((coef_in, coef), (s5_in, s5), (s3_in, s3), (rhs_in, res), (ends_in, ends), (s1_in, s1))
     loads = [pltpu.make_async_copy(src, dst, load.at[n]) for n, (src, dst) in enumerate(pairs)]
     for copy in loads:
         copy.start()
+    ytile[...] = jnp.zeros_like(ytile)
+    dtile[...] = jnp.zeros_like(dtile)
     loads[0].wait()
-    pl.semaphore_wait(barrier, sum(there.astype(jnp.int32) for _, _, there in sides))
+    pl.semaphore_wait(barrier, sum(there.astype(jnp.int32) for _, there in peers))
 
     def coef_copy(k, arriving):
         here = k if arriving else k ^ 1
@@ -180,23 +213,70 @@
 
         lax.fori_loop(0, q, body, 0)
 
-    invert(Q5, inv5)
     invert(Q3, inv3)
     invert(Q1, inv1)
 
+    def pack_rows(q, source, target):
+        for i in range(q):
+            target[0, pl.ds(i * NY, q), :] = source[pl.ds(i * q * q * NY, q, stride=NY), :]
+            target[1, pl.ds(i * NY, q), :] = source[pl.ds((i * q * q + q * (q - 1)) * NY + NY - 1, q, stride=NY), :]
+
+    pack_rows(Q3, inv3, gp3)
+    pack_rows(Q1, inv1, gp1)
+
+    def greet_copy(k, n, arriving):
+        here = k if arriving else k ^ 1
+        if n == 0:
+            src, dst = weights.at[pl.ds(2 if k < 2 else 0, 2)], gw.at[here]
+        elif k < 2:
+            q, inv, target = ((Q3, inv3, gx3), (Q1, inv1, gx1))[n - 1]
+            src, dst = inv.at[pl.ds(k * (q**3 - q * q) * NY, q * q * NY), :], target.at[here]
+        else:
+            source, target = ((gp3, gy3), (gp1, gy1))[n - 1]
+            src, dst = source.at[k - 2], target.at[here - 2]
+        return pltpu.make_async_remote_copy(
+            src_ref=src, dst_ref=dst, send_sem=gs.at[k, n], recv_sem=gr.at[here, n],
+            device_id={sides[k][0]: sides[k][1]}, device_id_type=MESH,
+        )
+
+    for k in (2, 3, 0, 1):
+
+        @pl.when(sides[k][2])
+        def _(k=k):
+            for n in range(3):
+                greet_copy(k, n, False).start()
+
+    invert(Q5, inv5)
+
+    def greeted():
+        for k in range(4):
+
+            @pl.when(sides[k][2])
+            def _(k=k):
+                for n in range(3):
+                    greet_copy(k, n, True).wait_recv()
+                    greet_copy(k, n, False).wait_send()
+
+    far = lax.rem(slab, 2)
+    near = 1 - far
+
     def lines(q):
+        if q < Q5:
+            return [(0, q)]
         return [(0, 1), (q - 1, 1)] + [(j, min(2, q - 1 - j)) for j in range(1, q - 1, 2)]
 
+    def face_at(k, q, first, count):
+        return pl.ds(pl.multiple_of(k * ((q**3 - q * q) * NY) + first * q * NY, NY), count * q * NY)
+
     def slab_copy(k, q, d, slot, piece, arriving):
-        first, count = lines(q)[piece]
-        size = count * q * NY
-        base = 0 if k == 0 else (q**3 - q * q) * NY
-        here = k if arriving else k ^ 1
+        first, count = (0, q) if piece is None else lines(q)[piece]
+        number = 0 if piece is None else piece
+        here = k if arriving else 1 - k
         return pltpu.make_async_remote_copy(
-            src_ref=d.at[slot, pl.ds(base + first * q * NY, size), :],
-            dst_ref=hx.at[slot, here, pl.ds(first * q * NY, size), :],
-            send_sem=xs.at[k, piece, slot], recv_sem=xr.at[here, piece, slot],
-            device_id={"slab": sides[k][1]}, device_id_type=MESH,
+            src_ref=d.at[slot, face_at(k, q, first, count), :],
+            dst_ref=hx.at[slot, here, pl.ds(first * q * NY, count * q * NY), :],
+            send_sem=xs.at[k, number, slot], recv_sem=xr.at[here, number, slot],
+            device_id={"slab": slab + 2 * k - 1}, device_id_type=MESH,
         )
 
     def cross_copy(k, q, slot, arriving):
@@ -208,7 +288,9 @@
         )
 
     def slab_do(k, method, *args):
-        @pl.when(sides[k][2])
+        index = slab + 2 * k - 1
+
+        @pl.when((index >= 0) & (index < ns))
         def _():
             getattr(slab_copy(k, *args), method)()
 
@@ -217,10 +299,12 @@
         def _():
             getattr(cross_copy(k, *args), method)()
 
-    def send_slab(q, d, slot, pieces):
+    def send_near(q, d, slot):
+        slab_do(near, "start", q, d, slot, None, False)
+
+    def send_far(q, d, slot, pieces):
         for piece in pieces:
-            for k in range(2):
-                slab_do(k, "start", q, d, slot, piece, False)
+            slab_do(far, "start", q, d, slot, piece, False)
 
     def send_cross(q, d, slot):
         for i in range(q):
@@ -229,9 +313,53 @@
         for k in range(2):
             cross_do(k, "start", q, slot, False)
 
-    def send_all(q, d, slot):
+    def corner_copy(g, slot, arriving):
+        here = g if arriving else 3 - g
+        return pltpu.make_async_remote_copy(
+            src_ref=dpack.at[slot, g], dst_ref=hd.at[slot, here],
+            send_sem=cs.at[g, slot], recv_sem=cr.at[here, slot],
+            device_id=corners[g][0], device_id_type=MESH,
+        )
+
+    def corner_do(g, method, *args):
+        @pl.when(corners[g][1])
+        def _():
+            getattr(corner_copy(g, *args), method)()
+
+    def send_corners(q, d, slot):
+        for g in range(4):
+            k, m = g // 2, g % 2
+            node = k * (q**3 - q * q) + m * (q * q - q)
+            dpack[slot, g, pl.ds(0, q), :] = d[slot, pl.ds(node * NY + m * (NY - 1), q, stride=NY), :]
+        for g in range(4):
+            corner_do(g, "start", slot, False)
+
+    def send_all(q, d, slot, with_corners):
+        if with_corners:
+            send_corners(q, d, slot)
         send_cross(q, d, slot)
-        send_slab(q, d, slot, range(len(lines(q))))
+        send_far(q, d, slot, range(len(lines(q))))
+        send_near(q, d, slot)
+
+    def arrived(q, d, slot, with_corners):
+        for k in range(2):
+            cross_do(k, "wait_recv", q, slot, True)
+        slab_do(near, "wait_recv", q, d, slot, None, True)
+        for piece in range(len(lines(q))):
+            slab_do(far, "wait_recv", q, d, slot, piece, True)
+        if with_corners:
+            for g in range(4):
+                corner_do(g, "wait_recv", slot, True)
+
+    def sent(q, d, slot, with_corners):
+        slab_do(near, "wait_send", q, d, slot, None, False)
+        for piece in range(len(lines(q))):
+            slab_do(far, "wait_send", q, d, slot, piece, False)
+        for k in range(2):
+            cross_do(k, "wait_send", q, slot, False)
+        if with_corners:
+            for g in range(4):
+                corner_do(g, "wait_send", slot, False)
 
     def product_wide(q, d, slot, t, high, low):
         count = q**3
@@ -259,10 +387,9 @@
                 total += s1[m, n] * parts[n]
             t[pl.ds(m * NY, NY), :] = total
 
-    def step(level, slot, a, b, update, send):
-        q, d, t, r, x, inv = (level[name] for name in ("q", "d", "t", "r", "x", "inv"))
+    def local_part(level, slot):
+        q, d, t, r = (level[name] for name in ("q", "d", "t", "r"))
         p = PENALTY[q]
-        other = 1 - slot
         level["product"](slot)
 
         def local(i, carry):
@@ -289,8 +416,8 @@
             at = pl.ds(0 if k == 0 else (q**3) * NY - face, face)
             r[at, :] = r[at, :] - (p * weights[k] * tiles(d[slot, at, :], q * q)).reshape(face, NZ)
 
-        for k in range(2):
-            cross_do(k, "wait_recv", q, slot, True)
+    def rims(level, slot, put):
+        q = level["q"]
         for i in range(q):
             ytile[0, pl.ds(i * q * NY, q, stride=NY), :] = hy[slot, 0, pl.ds(i * NY, q), :]
             ytile[1, pl.ds(i * q * NY + NY - 1, q, stride=NY), :] = hy[slot, 1, pl.ds(i * NY, q), :]
@@ -298,11 +425,28 @@
         def rim(i, carry):
             for k in range(2):
                 at = pl.ds(pl.multiple_of(i * (q * q * NY) + k * q * (q - 1) * NY, NY), q * NY)
-                part = p * weights[2 + k] * tiles(ytile[k, pl.ds(pl.multiple_of(i * (q * NY), NY), q * NY), :], q)
-                r[at, :] = r[at, :] + part.reshape(q * NY, NZ)
+                part = PENALTY[q] * weights[2 + k] * tiles(ytile[k, pl.ds(pl.multiple_of(i * (q * NY), NY), q * NY), :], q)
+                put(at, part.reshape(q * NY, NZ))
             return carry
 
         lax.fori_loop(0, q, rim, 0)
+
+    def slab_term(level, slot, k, first, count):
+        q = level["q"]
+        part = PENALTY[q] * weights[k] * tiles(hx[slot, k, pl.ds(first * q * NY, count * q * NY), :], count * q)
+        return part.reshape(count * q * NY, NZ)
+
+    def step(level, slot, a, b, update, send):
+        q, d, r, x, inv = (level[name] for name in ("q", "d", "r", "x", "inv"))
+        other = lax.rem(slot + 1, SLOTS)
+
+        def put(at, part):
+            r[at, :] = r[at, :] + part
+
+        local_part(level, slot)
+        for k in range(2):
+            cross_do(k, "wait_recv", q, slot, True)
+        rims(level, slot, put)
 
         def advance(at):
             value = a * d[slot, at, :] + b * inv[at, :] * r[at, :]
@@ -317,29 +461,100 @@
 
             lax.fori_loop(1, q - 1, inside, 0)
 
+        def slab_face(k, first, count):
+            at = face_at(k, q, first, count)
+            put(at, slab_term(level, slot, k, first, count))
+            if update:
+                advance(at)
+
+        slab_do(near, "wait_recv", q, d, slot, None, True)
+        slab_face(near, 0, q)
+        if send:
+            send_near(q, d, other)
         pieces = lines(q)
-        groups = [[0, 1]] + [[n] for n in range(2, len(pieces))]
+        groups = [[0, 1]] + [[n] for n in range(2, len(pieces))] if len(pieces) > 1 else [[0]]
         for number, group in enumerate(groups):
             for piece in group:
-                first, count = pieces[piece]
-                size = count * q * NY
-                for k in range(2):
-                    slab_do(k, "wait_recv", q, d, slot, piece, True)
-                    at = pl.ds((0 if k == 0 else (q**3 - q * q) * NY) + first * q * NY, size)
-                    part = p * weights[k] * tiles(hx[slot, k, pl.ds(first * q * NY, size), :], count * q)
-                    r[at, :] = r[at, :] + part.reshape(size, NZ)
-                    if update:
-                        advance(at)
+                slab_do(far, "wait_recv", q, d, slot, piece, True)
+                slab_face(far, *pieces[piece])
             if send:
                 if number == 0:
                     send_cross(q, d, other)
-                send_slab(q, d, other, group)
+                send_far(q, d, other, group)
+        sent(q, d, slot, False)
+
+    def correct(level, slot, other, b):
+        q, d, gx, gy = (level[name] for name in ("q", "d", "gx", "gy"))
+        p = PENALTY[q]
+        face = q * q * NY
         for k in range(2):
-            cross_do(k, "wait_send", q, slot, False)
-            for piece in range(len(pieces)):
-                slab_do(k, "wait_send", q, d, slot, piece, False)
-
-    def first_update(level, slot, factor):
+            for m in range(2):
+                dtile[m, pl.ds(m * (NY - 1), q, stride=NY), :] = hd[slot, 2 * k + m, pl.ds(0, q), :]
+            term = p * weights[k] * tiles(d[slot, pl.ds(k * (q**3 - q * q) * NY, face), :], q, q)
+            low, high = (p * gw[k, m] * tiles(dtile[m, pl.ds(0, q * NY), :], q) for m in range(2))
+            first, last = term[0:1] + low[None], term[q - 1 : q] + high[None]
+            term = jnp.concatenate([first, term[1 : q - 1], last] if q > 2 else [first, last], 0)
+            at = pl.ds(0, face)
+            hx[other, k, at, :] = hx[other, k, at, :] + b * gx[k, at, :] * term.reshape(face, NZ)
+        for m in range(2):
+            mine, theirs = pl.ds(m * (NY - 1), 1), pl.ds((1 - m) * (NY - 1), 1)
+            for i in range(q):
+                at = pl.ds(i * NY, q)
+                term = p * weights[2 + m, mine, :] * pack[slot, m, at, :]
+                for k in range(2):
+                    if i == k * (q - 1):
+                        term = term + p * gw[2 + m, k, theirs, :] * hd[slot, 2 * k + m, pl.ds(0, q), :]
+                hy[other, m, at, :] = hy[other, m, at, :] + b * gy[m, at, :] * term
+
+    def double_step(level, slot, first, second, with_corners):
+        q, d, r, x, inv = (level[name] for name in ("q", "d", "r", "x", "inv"))
+        other, third = lax.rem(slot + 1, SLOTS), lax.rem(slot + 2, SLOTS)
+
+        def planes(body):
+            def one_plane(i, carry):
+                body(plane_at(i, q))
+                return carry
+
+            lax.fori_loop(0, q, one_plane, 0)
+
+        def partial_next(at):
+            d[other, at, :] = first[0] * d[slot, at, :] + first[1] * inv[at, :] * r[at, :]
+
+        def put_both(at, part):
+            r[at, :] = r[at, :] + part
+            d[other, at, :] = d[other, at, :] + first[1] * inv[at, :] * part
+
+        def put(at, part):
+            r[at, :] = r[at, :] + part
+
+        def add(at):
+            x[at, :] = x[at, :] + d[other, at, :]
+
+        def advance(at):
+            value = second[0] * d[other, at, :] + second[1] * inv[at, :] * r[at, :]
+            d[third, at, :] = value
+            x[at, :] = x[at, :] + value
+
+        local_part(level, slot)
+        planes(partial_next)
+        send_all(q, d, other, False)
+        arrived(q, d, slot, True)
+        sent(q, d, other, False)
+        rims(level, slot, put_both)
+        for k in range(2):
+            put_both(face_at(k, q, 0, q), slab_term(level, slot, k, 0, q))
+        planes(add)
+        local_part(level, other)
+        arrived(q, d, other, False)
+        correct(level, slot, other, first[1])
+        rims(level, other, put)
+        for k in range(2):
+            put(face_at(k, q, 0, q), slab_term(level, other, k, 0, q))
+        planes(advance)
+        send_all(q, d, third, with_corners)
+        sent(q, d, slot, True)
+
+    def first_update(level, slot, factor, with_corners):
         q, d, x, r, inv = (level[name] for name in ("q", "d", "x", "r", "inv"))
 
         def body(i, carry):
@@ -350,7 +565,7 @@
             return carry
 
         lax.fori_loop(0, q, body, 0)
-        send_all(q, d, slot)
+        send_all(q, d, slot, with_corners)
 
     def pick(k, values):
         out = jnp.float32(values[0])
@@ -363,11 +578,29 @@
 
         def body(k, carry):
             a, b = pick(k, [f[0] for f in factors]), pick(k, [f[1] for f in factors])
-            step(level, lax.rem(exchange + k, 2), a, b, True, True)
+            step(level, lax.rem(exchange + k, SLOTS), a, b, True, True)
             return carry
 
         lax.fori_loop(0, loop, body, 0)
-        slot = (exchange + loop) % 2
+        slot = (exchange + loop) % SLOTS
+        if last:
+            step(level, slot, 0.0, 0.0, False, False)
+        else:
+            step(level, slot, *factors[-1], True, False)
+
+    def run_doubled(level, exchange, factors, last):
+        loop = (len(factors) - (0 if last else 1)) // 2
+
+        def body(k, carry):
+            first = [pick(k, [f[n] for f in factors[: 2 * loop : 2]]) for n in range(2)]
+            second = [pick(k, [f[n] for f in factors[1 : 2 * loop : 2]]) for n in range(2)]
+            double_step(level, lax.rem(exchange + 2 * k, SLOTS), first, second, True)
+            return carry
+
+        if loop > 1:
+            lax.fori_loop(0, loop - 1, body, 0)
+        double_step(level, (exchange + 2 * loop - 2) % SLOTS, *factors[2 * loop - 2 : 2 * loop], False)
+        slot = (exchange + 2 * loop) % SLOTS
         if last:
             step(level, slot, 0.0, 0.0, False, False)
         else:
@@ -396,7 +629,7 @@
 
         lax.fori_loop(0, qc, gather, 0)
 
-    def prolong(coarse, fine, slot, sum_into, qf, qc):
+    def prolong(coarse, fine, slot, sum_into, qf, qc, with_corners):
         table = lagrange(qf, qc)
 
         def spread(a, carry):
@@ -423,25 +656,26 @@
             return carry
 
         lax.fori_loop(0, qf, body, 0)
-        send_all(qf, fine, slot)
+        send_all(qf, fine, slot, with_corners)
 
     five = dict(q=Q5, d=d5, t=t5, r=res, x=sol, inv=inv5, product=lambda slot: product_wide(Q5, d5, slot, t5, sh5, sl5))
-    three = dict(q=Q3, d=d3, t=t3, r=r3, x=x3, inv=inv3, product=lambda slot: product_wide(Q3, d3, slot, t3, sh3, sl3))
-    one = dict(q=Q1, d=d1, t=t1, r=r1, x=x1, inv=inv1, product=lambda slot: product_small(d1, slot, t1))
+    three = dict(q=Q3, d=d3, t=t3, r=r3, x=x3, inv=inv3, gx=gx3, gy=gy3, product=lambda slot: product_wide(Q3, d3, slot, t3, sh3, sl3))
+    one = dict(q=Q1, d=d1, t=t1, r=r1, x=x1, inv=inv1, gx=gx1, gy=gy1, product=lambda slot: product_small(d1, slot, t1))
 
     first, pairs = chebyshev_factors(DEGREE, LAMBDA_TOP / 8.0)
     coarse_first, coarse_pairs = chebyshev_factors(COARSE_ITERS, LAMBDA_TOP / 40.0)
-    first_update(five, 0, first)
+    first_update(five, 0, first, False)
     run(five, 0, pairs, True)
     restrict(res, r3, Q5, Q3)
-    first_update(three, 1, first)
-    run(three, 3, pairs, True)
+    first_update(three, 3, first, True)
+    greeted()
+    run_doubled(three, 3, pairs, True)
     restrict(r3, r1, Q3, Q1)
-    first_update(one, 0, coarse_first)
-    run(one, 6, coarse_pairs, False)
-    prolong(x1, d3, 1, x3, Q3, Q1)
-    run(three, 13, [(0.0, first)] + pairs, False)
-    prolong(x3, d5, 0, sol, Q5, Q3)
+    first_update(one, 6 % SLOTS, coarse_first, True)
+    run_doubled(one, 6, coarse_pairs, False)
+    prolong(x1, d3, 13 % SLOTS, x3, Q3, Q1, True)
+    run_doubled(three, 13, [(0.0, first)] + pairs, False)
+    prolong(x3, d5, 16 % SLOTS, sol, Q5, Q3, False)
     run(five, 16, [(0.0, first)] + pairs, True)
 
 
@@ -451,7 +685,8 @@
     vmem = pl.BlockSpec(memory_space=pltpu.VMEM)
     hbm = pl.BlockSpec(memory_space=pltpu.HBM)
     field = lambda n: pltpu.VMEM((n, NZ), F32)
-    pair = lambda n: pltpu.VMEM((2, n, NZ), F32)
+    slots = lambda *n: pltpu.VMEM((SLOTS, *n, NZ), F32)
+    two = lambda n: pltpu.VMEM((2, n, NZ), F32)
     dma = pltpu.SemaphoreType.DMA
     sol, res = pl.pallas_call(
         kernel,
@@ -461,22 +696,30 @@
         scratch_shapes=[
             field(NY), pltpu.SMEM((2, NY), jnp.int32), pltpu.VMEM((Q5**3, Q5**3), F32), pltpu.VMEM((Q3**3, Q3**3), F32),
             pltpu.SMEM((Q1**3, Q1**3), F32),
-            pair(n5), field(n5), field(n5),
-            field(n3), field(n3), pair(n3), field(n3), field(n3),
-            field(n1), field(n1), pair(n1), field(n1), field(n1),
+            slots(n5), field(n5), field(n5),
+            field(n3), field(n3), slots(n3), field(n3), field(n3),
+            field(n1), field(n1), slots(n1), field(n1), field(n1),
             pltpu.VMEM((224, 224), BF16), pltpu.VMEM((224, 224), BF16),
             pltpu.VMEM((64, 64), BF16), pltpu.VMEM((64, 64), BF16),
             field(6 * 16 * NY), pltpu.VMEM((6, NY, NZ), F32),
-            pltpu.VMEM((2, 2, Q5 * Q5 * NY, NZ), F32), pltpu.VMEM((2, 2, Q5 * NY, NZ), F32),
-            pltpu.VMEM((2, Q5 * Q5 * NY, NZ), F32), pltpu.VMEM((2, 2, Q5 * NY, NZ), F32), pltpu.VMEM((4, NY, NZ), F32),
-            dma((2, 4, 2)), dma((2, 4, 2)), dma((2, 2)), dma((2, 2)), dma((4,)), dma((4,)), dma((6,)),
+            slots(2, Q5 * Q5 * NY), slots(2, Q5 * NY), two(Q5 * Q5 * NY), slots(2, Q5 * NY), pltpu.VMEM((4, NY, NZ), F32),
+            slots(4, NY), slots(4, NY), two(Q3 * NY),
+            two(Q3 * Q3 * NY), two(Q1 * Q1 * NY), two(Q3 * NY), two(Q1 * NY), two(Q3 * NY), two(Q1 * NY),
+            pltpu.VMEM((4, 2, NY, NZ), F32),
+            dma((2, 4, SLOTS)), dma((2, 4, SLOTS)), dma((2, SLOTS)), dma((2, SLOTS)), dma((4, SLOTS)), dma((4, SLOTS)),
+            dma((4, 3)), dma((4, 3)), dma((4,)), dma((4,)), dma((6,)),
         ],
         compiler_params=pltpu.CompilerParams(
             collective_id=0, has_side_effects=True, vmem_limit_bytes=48 * 2**20
         ),
     )(
-        coefficient.reshape(NY, NZ), bottom_top.reshape(2, NY), right_side.reshape(n5, NZ),
-        stiff_five, stiff_three, stiff_one,
+        *(
+            pltpu.with_memory_space_constraint(value, pltpu.HBM)
+            for value in (
+                coefficient.reshape(NY, NZ), bottom_top.reshape(2, NY), right_side.reshape(n5, NZ),
+                stiff_five, stiff_three, stiff_one,
+            )
+        )
     )
     return sol.reshape(shape), res.reshape(shape)
 

time: 104 us -> 88.6 us (0.85); the launches traced: 102 us -> 88.3 us
  Pallas kernels: 95.4 us -> 85.9 us
  local copies, waits for them, and re-layouts: 6.05 us -> 1.83 us
    pallas_call x1, Pallas kernels: 95.4 us -> 85.9 us  [per_device(): pl.pallas_call(kernel, out_shape=[jax.ShapeDtypeStruct((n5, NZ), F32)] *...]
    unnamed x14 -> x2, local copies, waits for them, and re-layouts: 6.05 us -> 1.83 us
where the time goes in v2:
time: 88.6 us; the launch traced here: 88.3 us
  Pallas kernels  85.9 us (97%)
  local copies, waits for them, and re-layouts  1.83 us (2%)
    pallas_call x1, Pallas kernels, per_device(): pl.pallas_call(kernel, out_shape=[jax.ShapeDtypeStruct((n5, NZ), F32)] *...  85.9 us
    unnamed x2, local copies, waits for them, and re-layouts  1.83 us

profile of v2, /device:TPU:13, one launch (start us, length us, event | category | flops | bytes accessed | tf_op | source)
XLA Modules:
  0.0 88.3 jit_solution(17953929025118258950)
XLA Ops:
  0.6 85.9 %shard_map.77 = (f32[1728,128]{1,0:T(8,128)S(1)}, f32[1728,128]{1,0:T(8,128)S(1)}) custom-call(f32[8,128]{1,0:T(8,128)} %bitcast.12, s32[2,8]{1,0:T(2,128)} %bitcast.13, f32[1728,128]{1,0:T(8,128)} %bitcast.11, f32[216,216]{1,0:T(8,128)} %s5_in.1, f32[64,64]{1,0:T(8,128)} %s3_in.1, f32[8,8]{1,0:T(8,128)} %s1_in.1), custom_call_target="tpu_custom_call" | custom-call | tf_op jit(solution)/shard_map/pallas_call | solution.py:691
  86.5 0.9 %copy.12 = f32[6,6,6,1,8,128]{5,4,3,2,1,0:T(8,128)} copy(f32[6,6,6,1,8,128]{5,4,3,2,1,0:T(8,128)S(1)} %bitcast.10) | data formatting | bytes 1769472
  87.4 0.9 %copy.13 = f32[6,6,6,1,8,128]{5,4,3,2,1,0:T(8,128)} copy(f32[6,6,6,1,8,128]{5,4,3,2,1,0:T(8,128)S(1)} %bitcast.9) | data formatting | bytes 1769472

commit v3 on v2

--- a/solution.py
+++ b/solution.py
@@ -63,7 +63,7 @@
     coef, ends, s5, s3, s1,
     d5, t5, inv5, x3, r3, d3, t3, inv3, x1, r1, d1, t1, inv1,
     sh5, sl5, sh3, sl3, work, weights, hx, hy, ytile, pack, hc,
-    hd, dpack, dtile, gx3, gx1, gy3, gy1, gp3, gp1, gw,
+    hd, dpack, dtile, gx3, gx1, gy3, gy1, gp3, gp1, gw, hxl, hyl,
     xs, xr, ys, yr, cs, cr, gs, gr, csem, crsem, load,
 ):
     slab, cross = lax.axis_index("slab"), lax.axis_index("cross")
@@ -416,11 +416,11 @@
             at = pl.ds(0 if k == 0 else (q**3) * NY - face, face)
             r[at, :] = r[at, :] - (p * weights[k] * tiles(d[slot, at, :], q * q)).reshape(face, NZ)
 
-    def rims(level, slot, put):
+    def rims(level, source, put):
         q = level["q"]
         for i in range(q):
-            ytile[0, pl.ds(i * q * NY, q, stride=NY), :] = hy[slot, 0, pl.ds(i * NY, q), :]
-            ytile[1, pl.ds(i * q * NY + NY - 1, q, stride=NY), :] = hy[slot, 1, pl.ds(i * NY, q), :]
+            ytile[0, pl.ds(i * q * NY, q, stride=NY), :] = source[0, pl.ds(i * NY, q), :]
+            ytile[1, pl.ds(i * q * NY + NY - 1, q, stride=NY), :] = source[1, pl.ds(i * NY, q), :]
 
         def rim(i, carry):
             for k in range(2):
@@ -431,9 +431,9 @@
 
         lax.fori_loop(0, q, rim, 0)
 
-    def slab_term(level, slot, k, first, count):
+    def slab_term(level, source, k, first, count):
         q = level["q"]
-        part = PENALTY[q] * weights[k] * tiles(hx[slot, k, pl.ds(first * q * NY, count * q * NY), :], count * q)
+        part = PENALTY[q] * weights[k] * tiles(source[k, pl.ds(first * q * NY, count * q * NY), :], count * q)
         return part.reshape(count * q * NY, NZ)
 
     def step(level, slot, a, b, update, send):
@@ -446,7 +446,7 @@
         local_part(level, slot)
         for k in range(2):
             cross_do(k, "wait_recv", q, slot, True)
-        rims(level, slot, put)
+        rims(level, hy.at[slot], put)
 
         def advance(at):
             value = a * d[slot, at, :] + b * inv[at, :] * r[at, :]
@@ -463,7 +463,7 @@
 
         def slab_face(k, first, count):
             at = face_at(k, q, first, count)
-            put(at, slab_term(level, slot, k, first, count))
+            put(at, slab_term(level, hx.at[slot], k, first, count))
             if update:
                 advance(at)
 
@@ -506,53 +506,118 @@
                         term = term + p * gw[2 + m, k, theirs, :] * hd[slot, 2 * k + m, pl.ds(0, q), :]
                 hy[other, m, at, :] = hy[other, m, at, :] + b * gy[m, at, :] * term
 
-    def double_step(level, slot, first, second, with_corners):
+    def planes(q, body):
+        def one_plane(i, carry):
+            body(plane_at(i, q))
+            return carry
+
+        lax.fori_loop(0, q, one_plane, 0)
+
+    def half_round(level, slot, a, b, total):
         q, d, r, x, inv = (level[name] for name in ("q", "d", "r", "x", "inv"))
-        other, third = lax.rem(slot + 1, SLOTS), lax.rem(slot + 2, SLOTS)
-
-        def planes(body):
-            def one_plane(i, carry):
-                body(plane_at(i, q))
-                return carry
-
-            lax.fori_loop(0, q, one_plane, 0)
+        other = lax.rem(slot + 1, SLOTS)
 
         def partial_next(at):
-            d[other, at, :] = first[0] * d[slot, at, :] + first[1] * inv[at, :] * r[at, :]
+            value = a * d[slot, at, :] + b * inv[at, :] * r[at, :]
+            d[other, at, :] = x[at, :] + value if total else value
 
         def put_both(at, part):
             r[at, :] = r[at, :] + part
-            d[other, at, :] = d[other, at, :] + first[1] * inv[at, :] * part
-
-        def put(at, part):
-            r[at, :] = r[at, :] + part
-
-        def add(at):
-            x[at, :] = x[at, :] + d[other, at, :]
-
-        def advance(at):
-            value = second[0] * d[other, at, :] + second[1] * inv[at, :] * r[at, :]
-            d[third, at, :] = value
-            x[at, :] = x[at, :] + value
+            d[other, at, :] = d[other, at, :] + b * inv[at, :] * part
 
         local_part(level, slot)
-        planes(partial_next)
+        planes(q, partial_next)
         send_all(q, d, other, False)
         arrived(q, d, slot, True)
         sent(q, d, other, False)
-        rims(level, slot, put_both)
-        for k in range(2):
-            put_both(face_at(k, q, 0, q), slab_term(level, slot, k, 0, q))
-        planes(add)
+        rims(level, hy.at[slot], put_both)
+        for k in range(2):
+            put_both(face_at(k, q, 0, q), slab_term(level, hx.at[slot], k, 0, q))
+
+    def double_step(level, slot, first, second, with_corners, total):
+        q, d, r, x, inv = (level[name] for name in ("q", "d", "r", "x", "inv"))
+        other, third = lax.rem(slot + 1, SLOTS), lax.rem(slot + 2, SLOTS)
+
+        def put(at, part):
+            r[at, :] = r[at, :] + part
+
+        def add(at):
+            x[at, :] = x[at, :] + d[other, at, :]
+
+        def advance(at):
+            value = second[0] * d[other, at, :] + second[1] * inv[at, :] * r[at, :]
+            if total:
+                d[third, at, :] = x[at, :] + value
+            else:
+                d[third, at, :] = value
+                x[at, :] = x[at, :] + value
+
+        half_round(level, slot, *first, False)
+        planes(q, add)
         local_part(level, other)
         arrived(q, d, other, False)
         correct(level, slot, other, first[1])
-        rims(level, other, put)
-        for k in range(2):
-            put(face_at(k, q, 0, q), slab_term(level, other, k, 0, q))
-        planes(advance)
+        rims(level, hy.at[other], put)
+        for k in range(2):
+            put(face_at(k, q, 0, q), slab_term(level, hx.at[other], k, 0, q))
+        planes(q, advance)
         send_all(q, d, third, with_corners)
         sent(q, d, slot, True)
+
+    def finish_round(level, slot, a, b):
+        q, d = level["q"], level["d"]
+        other = lax.rem(slot + 1, SLOTS)
+        half_round(level, slot, a, b, True)
+        arrived(q, d, other, False)
+        correct(level, slot, other, b)
+        sent(q, d, slot, True)
+
+    def lift_faces(qc, qf, slot):
+        table = lagrange(qf, qc)
+        spread = []
+        for e in range(qc):
+            column = jnp.zeros((NY, NZ), F32)
+            for n in range(qf):
+                if table[n, e] != 0.0:
+                    column = jnp.where(row == n, float(table[n, e]), column)
+            spread.append(column)
+        for k in range(2):
+            lines_in = tiles(hx[slot, k, pl.ds(0, qc * qc * NY), :], qc, qc)
+            for j in range(qf):
+                line = weighted(table[j], [lines_in[n] for n in range(qc)])
+                for n in range(qf):
+                    hxl[k, pl.ds((j * qf + n) * NY, NY), :] = weighted(table[n], [line[e] for e in range(qc)])
+            for i in range(qf):
+                line = weighted(table[i], [hy[slot, k, pl.ds(a * NY, qc), :] for a in range(qc)])
+                value = spread[0] * line[0:1]
+                for e in range(1, qc):
+                    value = value + spread[e] * line[e : e + 1]
+                hyl[k, pl.ds(i * NY, NY), :] = value
+
+    def lifted_step(coarse, slot, level, here, factor, awaited, with_corners):
+        q, d, r, x, inv = (level[name] for name in ("q", "d", "r", "x", "inv"))
+        following = (here + 1) % SLOTS
+        prolong(coarse["d"].at[slot], d, here, x, q, coarse["q"])
+        local_part(level, here)
+        if awaited:
+            arrived(coarse["q"], coarse["d"], slot, False)
+        lift_faces(coarse["q"], q, slot)
+
+        def put(at, part):
+            r[at, :] = r[at, :] + part
+
+        def advance(at):
+            value = factor * inv[at, :] * r[at, :]
+            d[following, at, :] = value
+            x[at, :] = x[at, :] + value
+
+        rims(level, hyl, put)
+        for k in range(2):
+            put(face_at(k, q, 0, q), slab_term(level, hxl, k, 0, q))
+        planes(q, advance)
+        send_all(q, d, following, with_corners)
+        if awaited:
+            sent(coarse["q"], coarse["d"], slot, False)
 
     def first_update(level, slot, factor, with_corners):
         q, d, x, r, inv = (level[name] for name in ("q", "d", "x", "r", "inv"))
@@ -583,24 +648,6 @@
 
         lax.fori_loop(0, loop, body, 0)
         slot = (exchange + loop) % SLOTS
-        if last:
-            step(level, slot, 0.0, 0.0, False, False)
-        else:
-            step(level, slot, *factors[-1], True, False)
-
-    def run_doubled(level, exchange, factors, last):
-        loop = (len(factors) - (0 if last else 1)) // 2
-
-        def body(k, carry):
-            first = [pick(k, [f[n] for f in factors[: 2 * loop : 2]]) for n in range(2)]
-            second = [pick(k, [f[n] for f in factors[1 : 2 * loop : 2]]) for n in range(2)]
-            double_step(level, lax.rem(exchange + 2 * k, SLOTS), first, second, True)
-            return carry
-
-        if loop > 1:
-            lax.fori_loop(0, loop - 1, body, 0)
-        double_step(level, (exchange + 2 * loop - 2) % SLOTS, *factors[2 * loop - 2 : 2 * loop], False)
-        slot = (exchange + 2 * loop) % SLOTS
         if last:
             step(level, slot, 0.0, 0.0, False, False)
         else:
@@ -629,7 +676,7 @@
 
         lax.fori_loop(0, qc, gather, 0)
 
-    def prolong(coarse, fine, slot, sum_into, qf, qc, with_corners):
+    def prolong(coarse, fine, slot, sum_into, qf, qc):
         table = lagrange(qf, qc)
 
         def spread(a, carry):
@@ -656,7 +703,6 @@
             return carry
 
         lax.fori_loop(0, qf, body, 0)
-        send_all(qf, fine, slot, with_corners)
 
     five = dict(q=Q5, d=d5, t=t5, r=res, x=sol, inv=inv5, product=lambda slot: product_wide(Q5, d5, slot, t5, sh5, sl5))
     three = dict(q=Q3, d=d3, t=t3, r=r3, x=x3, inv=inv3, gx=gx3, gy=gy3, product=lambda slot: product_wide(Q3, d3, slot, t3, sh3, sl3))
@@ -669,14 +715,22 @@
     restrict(res, r3, Q5, Q3)
     first_update(three, 3, first, True)
     greeted()
-    run_doubled(three, 3, pairs, True)
+    double_step(three, 3, *pairs, False, False)
+    step(three, 5 % SLOTS, 0.0, 0.0, False, False)
     restrict(r3, r1, Q3, Q1)
     first_update(one, 6 % SLOTS, coarse_first, True)
-    run_doubled(one, 6, coarse_pairs, False)
-    prolong(x1, d3, 13 % SLOTS, x3, Q3, Q1, True)
-    run_doubled(three, 13, [(0.0, first)] + pairs, False)
-    prolong(x3, d5, 16 % SLOTS, sol, Q5, Q3, False)
-    run(five, 16, [(0.0, first)] + pairs, True)
+
+    def coarse_rounds(n, carry):
+        factors = [[pick(n, [f[part] for f in coarse_pairs[half:6:2]]) for part in range(2)] for half in range(2)]
+        double_step(one, lax.rem(6 + 2 * n, SLOTS), *factors, True, False)
+        return carry
+
+    lax.fori_loop(0, 3, coarse_rounds, 0)
+    finish_round(one, 12 % SLOTS, *coarse_pairs[6])
+    lifted_step(one, 13 % SLOTS, three, 13 % SLOTS, first, False, True)
+    double_step(three, 14 % SLOTS, *pairs, False, True)
+    lifted_step(three, 16 % SLOTS, five, 16 % SLOTS, first, True, False)
+    run(five, 17, pairs, True)
 
 
 def per_device(right_side, coefficient, bottom_top, stiff_five, stiff_three, stiff_one):
@@ -705,7 +759,7 @@
             slots(2, Q5 * Q5 * NY), slots(2, Q5 * NY), two(Q5 * Q5 * NY), slots(2, Q5 * NY), pltpu.VMEM((4, NY, NZ), F32),
             slots(4, NY), slots(4, NY), two(Q3 * NY),
             two(Q3 * Q3 * NY), two(Q1 * Q1 * NY), two(Q3 * NY), two(Q1 * NY), two(Q3 * NY), two(Q1 * NY),
-            pltpu.VMEM((4, 2, NY, NZ), F32),
+            pltpu.VMEM((4, 2, NY, NZ), F32), two(Q5 * Q5 * NY), two(Q5 * NY),
             dma((2, 4, SLOTS)), dma((2, 4, SLOTS)), dma((2, SLOTS)), dma((2, SLOTS)), dma((4, SLOTS)), dma((4, SLOTS)),
             dma((4, 3)), dma((4, 3)), dma((4,)), dma((4,)), dma((6,)),
         ],

time: 88.6 us -> 86.6 us (0.977); the launches traced: 88.3 us -> 85.4 us
  Pallas kernels: 85.9 us -> 82.9 us
    pallas_call x1, Pallas kernels: 85.9 us -> 82.9 us  [per_device(): pl.pallas_call(kernel, out_shape=[jax.ShapeDtypeStruct((n5, NZ), F32)] *...]
where the time goes in v3:
time: 86.6 us; the launch traced here: 85.4 us
  Pallas kernels  82.9 us (96%)
  local copies, waits for them, and re-layouts  1.83 us (2%)
    pallas_call x1, Pallas kernels, per_device(): pl.pallas_call(kernel, out_shape=[jax.ShapeDtypeStruct((n5, NZ), F32)] *...  82.9 us
    unnamed x2, local copies, waits for them, and re-layouts  1.83 us

profile of v3, /device:TPU:13, one launch (start us, length us, event | category | flops | bytes accessed | tf_op | source)
XLA Modules:
  0.0 85.4 jit_solution(13593883308846919872)
XLA Ops:
  0.6 82.9 %shard_map.77 = (f32[1728,128]{1,0:T(8,128)S(1)}, f32[1728,128]{1,0:T(8,128)S(1)}) custom-call(f32[8,128]{1,0:T(8,128)} %bitcast.12, s32[2,8]{1,0:T(2,128)} %bitcast.13, f32[1728,128]{1,0:T(8,128)} %bitcast.11, f32[216,216]{1,0:T(8,128)} %s5_in.1, f32[64,64]{1,0:T(8,128)} %s3_in.1, f32[8,8]{1,0:T(8,128)} %s1_in.1), custom_call_target="tpu_custom_call" | custom-call | tf_op jit(solution)/shard_map/pallas_call | solution.py:745
  83.6 0.9 %copy.12 = f32[6,6,6,1,8,128]{5,4,3,2,1,0:T(8,128)} copy(f32[6,6,6,1,8,128]{5,4,3,2,1,0:T(8,128)S(1)} %bitcast.10) | data formatting | bytes 1769472
  84.5 0.9 %copy.13 = f32[6,6,6,1,8,128]{5,4,3,2,1,0:T(8,128)} copy(f32[6,6,6,1,8,128]{5,4,3,2,1,0:T(8,128)S(1)} %bitcast.9) | data formatting | bytes 1769472

commit v4 on v3

--- a/solution.py
+++ b/solution.py
@@ -58,12 +58,20 @@
     return value.reshape(*lead, NY, NZ)
 
 
+class Unslotted:
+    def __init__(self, ref):
+        self.ref, self.at = ref, self
+
+    def __getitem__(self, index):
+        return self.ref.at[index[1:]]
+
+
 def kernel(
     coef_in, ends_in, rhs_in, s5_in, s3_in, s1_in, sol, res,
-    coef, ends, s5, s3, s1,
+    mine, ends, s5, s3, s1,
     d5, t5, inv5, x3, r3, d3, t3, inv3, x1, r1, d1, t1, inv1,
     sh5, sl5, sh3, sl3, work, weights, hx, hy, ytile, pack, hc,
-    hd, dpack, dtile, gx3, gx1, gy3, gy1, gp3, gp1, gw, hxl, hyl,
+    hd, dpack, dtile, gx3, gx1, gy3, gy1, gp3, gp1, gw, hxl, hyl, hcc, gx5, gy5,
     xs, xr, ys, yr, cs, cr, gs, gr, csem, crsem, load,
 ):
     slab, cross = lax.axis_index("slab"), lax.axis_index("cross")
@@ -103,6 +111,7 @@
 
         @pl.when(jnp.logical_not(corners[g][1]))
         def _(g=g):
+            hcc[g] = jnp.zeros_like(hcc[g])
             for slot in range(SLOTS):
                 hd[slot, g] = jnp.zeros_like(hd[slot, g])
 
@@ -114,30 +123,162 @@
         def _(device=device):
             pl.semaphore_signal(barrier, inc=1, device_id=device, device_id_type=MESH)
 
-    pairs = ((coef_in, coef), (s5_in, s5), (s3_in, s3), (rhs_in, res), (ends_in, ends), (s1_in, s1))
+    pairs = ((coef_in, mine.at[0]), (s5_in, s5), (s3_in, s3), (rhs_in, res), (ends_in, ends), (s1_in, s1))
     loads = [pltpu.make_async_copy(src, dst, load.at[n]) for n, (src, dst) in enumerate(pairs)]
     for copy in loads:
         copy.start()
     ytile[...] = jnp.zeros_like(ytile)
     dtile[...] = jnp.zeros_like(dtile)
-    loads[0].wait()
-    pl.semaphore_wait(barrier, sum(there.astype(jnp.int32) for _, there in peers))
-
-    def coef_copy(k, arriving):
+    for copy in loads:
+        copy.wait()
+
+    row = lax.broadcasted_iota(jnp.int32, (NY, NZ), 0)
+    lane = lax.broadcasted_iota(jnp.int32, (NY, NZ), 1)
+    bottom = jnp.zeros((NY, NZ), F32)
+    top = jnp.zeros((NY, NZ), F32)
+    for y in range(NY):
+        bottom = jnp.where(row == y, ends[0, y].astype(F32), bottom)
+        top = jnp.where(row == y, ends[1, y].astype(F32), top)
+    mine[1] = jnp.where(lane == 0, bottom, jnp.where(lane == NZ - 1, top, 0.0))
+
+    far = lax.rem(slab, 2)
+    near = 1 - far
+
+    def lines(q):
+        if q < Q5:
+            return [(0, q)]
+        return [(0, 1), (q - 1, 1)] + [(j, min(2, q - 1 - j)) for j in range(1, q - 1, 2)]
+
+    def face_at(k, q, first, count):
+        return pl.ds(pl.multiple_of(k * ((q**3 - q * q) * NY) + first * q * NY, NY), count * q * NY)
+
+    def slab_copy(k, q, d, slot, piece, arriving):
+        first, count = (0, q) if piece is None else lines(q)[piece]
+        number = 0 if piece is None else piece
+        here = k if arriving else 1 - k
+        return pltpu.make_async_remote_copy(
+            src_ref=d.at[slot, face_at(k, q, first, count), :],
+            dst_ref=hx.at[slot, here, pl.ds(first * q * NY, count * q * NY), :],
+            send_sem=xs.at[k, number, slot], recv_sem=xr.at[here, number, slot],
+            device_id={"slab": slab + 2 * k - 1}, device_id_type=MESH,
+        )
+
+    def cross_copy(k, q, slot, arriving):
         here = k if arriving else k ^ 1
         return pltpu.make_async_remote_copy(
-            src_ref=coef, dst_ref=hc.at[here], send_sem=csem.at[k], recv_sem=crsem.at[here],
-            device_id={sides[k][0]: sides[k][1]}, device_id_type=MESH,
+            src_ref=pack.at[slot, k, pl.ds(0, q * NY), :], dst_ref=hy.at[slot, here, pl.ds(0, q * NY), :],
+            send_sem=ys.at[k, slot], recv_sem=yr.at[here, slot],
+            device_id={"cross": sides[2 + k][1]}, device_id_type=MESH,
         )
 
-    for k in range(4):
-
-        @pl.when(sides[k][2])
+    def slab_do(k, method, *args):
+        index = slab + 2 * k - 1
+
+        @pl.when((index >= 0) & (index < ns))
+        def _():
+            getattr(slab_copy(k, *args), method)()
+
+    def cross_do(k, method, *args):
+        @pl.when(sides[2 + k][2])
+        def _():
+            getattr(cross_copy(k, *args), method)()
+
+    def send_near(q, d, slot):
+        slab_do(near, "start", q, d, slot, None, False)
+
+    def send_far(q, d, slot, pieces):
+        for piece in pieces:
+            slab_do(far, "start", q, d, slot, piece, False)
+
+    def send_cross(q, d, slot):
+        for i in range(q):
+            pack[slot, 0, pl.ds(i * NY, q), :] = d[slot, pl.ds(i * q * q * NY, q, stride=NY), :]
+            pack[slot, 1, pl.ds(i * NY, q), :] = d[slot, pl.ds((i * q * q + q * (q - 1)) * NY + NY - 1, q, stride=NY), :]
+        for k in range(2):
+            cross_do(k, "start", q, slot, False)
+
+    def corner_copy(g, slot, arriving):
+        here = g if arriving else 3 - g
+        return pltpu.make_async_remote_copy(
+            src_ref=dpack.at[slot, g], dst_ref=hd.at[slot, here],
+            send_sem=cs.at[g, slot], recv_sem=cr.at[here, slot],
+            device_id=corners[g][0], device_id_type=MESH,
+        )
+
+    def corner_do(g, method, *args):
+        @pl.when(corners[g][1])
+        def _():
+            getattr(corner_copy(g, *args), method)()
+
+    def send_corners(q, d, slot):
+        for g in range(4):
+            k, m = g // 2, g % 2
+            node = k * (q**3 - q * q) + m * (q * q - q)
+            dpack[slot, g, pl.ds(0, q), :] = d[slot, pl.ds(node * NY + m * (NY - 1), q, stride=NY), :]
+        for g in range(4):
+            corner_do(g, "start", slot, False)
+
+    def send_all(q, d, slot, with_corners):
+        if with_corners:
+            send_corners(q, d, slot)
+        send_cross(q, d, slot)
+        send_far(q, d, slot, range(len(lines(q))))
+        send_near(q, d, slot)
+
+    def arrived_cross(q, slot):
+        for k in range(2):
+            cross_do(k, "wait_recv", q, slot, True)
+
+    def arrived_slab(q, d, slot):
+        slab_do(near, "wait_recv", q, d, slot, None, True)
+        for piece in range(len(lines(q))):
+            slab_do(far, "wait_recv", q, d, slot, piece, True)
+
+    def arrived_corners(slot):
+        for g in range(4):
+            corner_do(g, "wait_recv", slot, True)
+
+    def sent(q, d, slot, with_corners):
+        slab_do(near, "wait_send", q, d, slot, None, False)
+        for piece in range(len(lines(q))):
+            slab_do(far, "wait_send", q, d, slot, piece, False)
+        for k in range(2):
+            cross_do(k, "wait_send", q, slot, False)
+        if with_corners:
+            for g in range(4):
+                corner_do(g, "wait_send", slot, False)
+
+    def pack_rows(q, source, target):
+        for i in range(q):
+            target[0, pl.ds(i * NY, q), :] = source[pl.ds(i * q * q * NY, q, stride=NY), :]
+            target[1, pl.ds(i * NY, q), :] = source[pl.ds((i * q * q + q * (q - 1)) * NY + NY - 1, q, stride=NY), :]
+
+    pack_rows(Q5, res, pack.at[0])
+    pl.semaphore_wait(barrier, sum(there.astype(jnp.int32) for _, there in peers))
+
+    def coef_copy(k, arriving):
+        if k < 4:
+            here = k if arriving else k ^ 1
+            src, dst = mine, hc.at[here]
+        else:
+            here = k if arriving else 11 - k
+            src, dst = mine.at[0], hcc.at[here - 4]
+        return pltpu.make_async_remote_copy(
+            src_ref=src, dst_ref=dst, send_sem=csem.at[k], recv_sem=crsem.at[here],
+            device_id=peers[k][0], device_id_type=MESH,
+        )
+
+    for k in (2, 3, 0, 1, 4, 5, 6, 7):
+
+        @pl.when(peers[k][1])
         def _(k=k):
             coef_copy(k, False).start()
 
-    for copy in loads[1:]:
-        copy.wait()
+    raw = Unslotted(res)
+    for k in range(2):
+        cross_do(k, "start", Q5, 0, False)
+    slab_do(far, "start", Q5, raw, 0, None, False)
+    slab_do(near, "start", Q5, raw, 0, None, False)
 
     def split(table, high, low, count):
         value = table[...]
@@ -162,30 +303,37 @@
     spread_diagonal(s3, inv3, Q3**3)
     for n in range(Q1**3):
         inv1[pl.ds(n * NY, NY), :] = jnp.full((NY, NZ), s1[n, n])
-
-    for k in range(4):
-
-        @pl.when(sides[k][2])
-        def _(k=k):
-            coef_copy(k, True).wait_recv()
-            coef_copy(k, False).wait_send()
-
-    row = lax.broadcasted_iota(jnp.int32, (NY, NZ), 0)
-    lane = lax.broadcasted_iota(jnp.int32, (NY, NZ), 1)
-    c = coef[...]
-    bottom = jnp.zeros((NY, NZ), F32)
-    top = jnp.zeros((NY, NZ), F32)
-    for y in range(NY):
-        bottom = jnp.where(row == y, ends[0, y].astype(F32), bottom)
-        top = jnp.where(row == y, ends[1, y].astype(F32), top)
-    y_before = jnp.where(row == 0, pltpu.roll(hc[2], 1, 0), pltpu.roll(c, 1, 0))
-    y_after = jnp.where(row == NY - 1, pltpu.roll(hc[3], NY - 1, 0), pltpu.roll(c, NY - 1, 0))
-    weights[0] = 0.5 * (c + hc[0])
-    weights[1] = 0.5 * (c + hc[1])
-    weights[2] = 0.5 * (c + y_before)
-    weights[3] = 0.5 * (c + y_after)
-    weights[4] = jnp.where(lane == 0, bottom * c, 0.5 * (c + pltpu.roll(c, 1, 1)))
-    weights[5] = jnp.where(lane == NZ - 1, top * c, 0.5 * (c + pltpu.roll(c, NZ - 1, 1)))
+    for k in range(2):
+        gx5[k] = inv5[face_at(1 - k, Q5, 0, Q5), :]
+        for i in range(Q5):
+            node = i * Q5 * Q5 + (1 - k) * Q5 * (Q5 - 1)
+            gy5[k, pl.ds(i * NY, Q5), :] = inv5[pl.ds(node * NY, Q5, stride=NY), :]
+
+    def coefs_done(ks):
+        for k in ks:
+
+            @pl.when(peers[k][1])
+            def _(k=k):
+                coef_copy(k, True).wait_recv()
+                coef_copy(k, False).wait_send()
+
+    coefs_done(range(4))
+    c = mine[0]
+
+    def cross_weights(own, below, above):
+        before = jnp.where(row == 0, pltpu.roll(below, 1, 0), pltpu.roll(own, 1, 0))
+        after = jnp.where(row == NY - 1, pltpu.roll(above, NY - 1, 0), pltpu.roll(own, NY - 1, 0))
+        return 0.5 * (own + before), 0.5 * (own + after)
+
+    def end_weights(own, flags):
+        low = jnp.where(lane == 0, flags * own, 0.5 * (own + pltpu.roll(own, 1, 1)))
+        high = jnp.where(lane == NZ - 1, flags * own, 0.5 * (own + pltpu.roll(own, NZ - 1, 1)))
+        return low, high
+
+    weights[0] = 0.5 * (c + hc[0, 0])
+    weights[1] = 0.5 * (c + hc[1, 0])
+    weights[2], weights[3] = cross_weights(c, hc[2, 0], hc[3, 0])
+    weights[4], weights[5] = end_weights(c, mine[1])
 
     def ends_added(base, q, y_pair, z_pair):
         first = base[0:1] + y_pair[0][None]
@@ -215,11 +363,6 @@
 
     invert(Q3, inv3)
     invert(Q1, inv1)
-
-    def pack_rows(q, source, target):
-        for i in range(q):
-            target[0, pl.ds(i * NY, q), :] = source[pl.ds(i * q * q * NY, q, stride=NY), :]
-            target[1, pl.ds(i * NY, q), :] = source[pl.ds((i * q * q + q * (q - 1)) * NY + NY - 1, q, stride=NY), :]
 
     pack_rows(Q3, inv3, gp3)
     pack_rows(Q1, inv1, gp1)
@@ -256,110 +399,6 @@
                 for n in range(3):
                     greet_copy(k, n, True).wait_recv()
                     greet_copy(k, n, False).wait_send()
-
-    far = lax.rem(slab, 2)
-    near = 1 - far
-
-    def lines(q):
-        if q < Q5:
-            return [(0, q)]
-        return [(0, 1), (q - 1, 1)] + [(j, min(2, q - 1 - j)) for j in range(1, q - 1, 2)]
-
-    def face_at(k, q, first, count):
-        return pl.ds(pl.multiple_of(k * ((q**3 - q * q) * NY) + first * q * NY, NY), count * q * NY)
-
-    def slab_copy(k, q, d, slot, piece, arriving):
-        first, count = (0, q) if piece is None else lines(q)[piece]
-        number = 0 if piece is None else piece
-        here = k if arriving else 1 - k
-        return pltpu.make_async_remote_copy(
-            src_ref=d.at[slot, face_at(k, q, first, count), :],
-            dst_ref=hx.at[slot, here, pl.ds(first * q * NY, count * q * NY), :],
-            send_sem=xs.at[k, number, slot], recv_sem=xr.at[here, number, slot],
-            device_id={"slab": slab + 2 * k - 1}, device_id_type=MESH,
-        )
-
-    def cross_copy(k, q, slot, arriving):
-        here = k if arriving else k ^ 1
-        return pltpu.make_async_remote_copy(
-            src_ref=pack.at[slot, k, pl.ds(0, q * NY), :], dst_ref=hy.at[slot, here, pl.ds(0, q * NY), :],
-            send_sem=ys.at[k, slot], recv_sem=yr.at[here, slot],
-            device_id={"cross": sides[2 + k][1]}, device_id_type=MESH,
-        )
-
-    def slab_do(k, method, *args):
-        index = slab + 2 * k - 1
-
-        @pl.when((index >= 0) & (index < ns))
-        def _():
-            getattr(slab_copy(k, *args), method)()
-
-    def cross_do(k, method, *args):
-        @pl.when(sides[2 + k][2])
-        def _():
-            getattr(cross_copy(k, *args), method)()
-
-    def send_near(q, d, slot):
-        slab_do(near, "start", q, d, slot, None, False)
-
-    def send_far(q, d, slot, pieces):
-        for piece in pieces:
-            slab_do(far, "start", q, d, slot, piece, False)
-
-    def send_cross(q, d, slot):
-        for i in range(q):
-            pack[slot, 0, pl.ds(i * NY, q), :] = d[slot, pl.ds(i * q * q * NY, q, stride=NY), :]
-            pack[slot, 1, pl.ds(i * NY, q), :] = d[slot, pl.ds((i * q * q + q * (q - 1)) * NY + NY - 1, q, stride=NY), :]
-        for k in range(2):
-            cross_do(k, "start", q, slot, False)
-
-    def corner_copy(g, slot, arriving):
-        here = g if arriving else 3 - g
-        return pltpu.make_async_remote_copy(
-            src_ref=dpack.at[slot, g], dst_ref=hd.at[slot, here],
-            send_sem=cs.at[g, slot], recv_sem=cr.at[here, slot],
-            device_id=corners[g][0], device_id_type=MESH,
-        )
-
-    def corner_do(g, method, *args):
-        @pl.when(corners[g][1])
-        def _():
-            getattr(corner_copy(g, *args), method)()
-
-    def send_corners(q, d, slot):
-        for g in range(4):
-            k, m = g // 2, g % 2
-            node = k * (q**3 - q * q) + m * (q * q - q)
-            dpack[slot, g, pl.ds(0, q), :] = d[slot, pl.ds(node * NY + m * (NY - 1), q, stride=NY), :]
-        for g in range(4):
-            corner_do(g, "start", slot, False)
-
-    def send_all(q, d, slot, with_corners):
-        if with_corners:
-            send_corners(q, d, slot)
-        send_cross(q, d, slot)
-        send_far(q, d, slot, range(len(lines(q))))
-        send_near(q, d, slot)
-
-    def arrived(q, d, slot, with_corners):
-        for k in range(2):
-            cross_do(k, "wait_recv", q, slot, True)
-        slab_do(near, "wait_recv", q, d, slot, None, True)
-        for piece in range(len(lines(q))):
-            slab_do(far, "wait_recv", q, d, slot, piece, True)
-        if with_corners:
-            for g in range(4):
-                corner_do(g, "wait_recv", slot, True)
-
-    def sent(q, d, slot, with_corners):
-        slab_do(near, "wait_send", q, d, slot, None, False)
-        for piece in range(len(lines(q))):
-            slab_do(far, "wait_send", q, d, slot, piece, False)
-        for k in range(2):
-            cross_do(k, "wait_send", q, slot, False)
-        if with_corners:
-            for g in range(4):
-                corner_do(g, "wait_send", slot, False)
 
     def product_wide(q, d, slot, t, high, low):
         count = q**3
@@ -483,7 +522,7 @@
                 send_far(q, d, other, group)
         sent(q, d, slot, False)
 
-    def correct(level, slot, other, b):
+    def correct(level, slot, b, slab_put, cross_put):
         q, d, gx, gy = (level[name] for name in ("q", "d", "gx", "gy"))
         p = PENALTY[q]
         face = q * q * NY
@@ -495,7 +534,7 @@
             first, last = term[0:1] + low[None], term[q - 1 : q] + high[None]
             term = jnp.concatenate([first, term[1 : q - 1], last] if q > 2 else [first, last], 0)
             at = pl.ds(0, face)
-            hx[other, k, at, :] = hx[other, k, at, :] + b * gx[k, at, :] * term.reshape(face, NZ)
+            slab_put(k, at, b * gx[k, at, :] * term.reshape(face, NZ))
         for m in range(2):
             mine, theirs = pl.ds(m * (NY - 1), 1), pl.ds((1 - m) * (NY - 1), 1)
             for i in range(q):
@@ -504,7 +543,7 @@
                 for k in range(2):
                     if i == k * (q - 1):
                         term = term + p * gw[2 + m, k, theirs, :] * hd[slot, 2 * k + m, pl.ds(0, q), :]
-                hy[other, m, at, :] = hy[other, m, at, :] + b * gy[m, at, :] * term
+                cross_put(m, at, b * gy[m, at, :] * term)
 
     def planes(q, body):
         def one_plane(i, carry):
@@ -528,9 +567,10 @@
         local_part(level, slot)
         planes(q, partial_next)
         send_all(q, d, other, False)
-        arrived(q, d, slot, True)
+        arrived_cross(q, slot)
         sent(q, d, other, False)
         rims(level, hy.at[slot], put_both)
+        arrived_slab(q, d, slot)
         for k in range(2):
             put_both(face_at(k, q, 0, q), slab_term(level, hx.at[slot], k, 0, q))
 
@@ -555,9 +595,21 @@
         half_round(level, slot, *first, False)
         planes(q, add)
         local_part(level, other)
-        arrived(q, d, other, False)
-        correct(level, slot, other, first[1])
+        arrived_corners(slot)
+
+        def keep_slab(k, at, part):
+            hxl[k, at, :] = part
+
+        def keep_cross(m, at, part):
+            hyl[m, at, :] = part
+
+        correct(level, slot, first[1], keep_slab, keep_cross)
+        rims(level, hyl, put)
+        for k in range(2):
+            put(face_at(k, q, 0, q), slab_term(level, hxl, k, 0, q))
+        arrived_cross(q, other)
         rims(level, hy.at[other], put)
+        arrived_slab(q, d, other)
         for k in range(2):
             put(face_at(k, q, 0, q), slab_term(level, hx.at[other], k, 0, q))
         planes(q, advance)
@@ -568,11 +620,29 @@
         q, d = level["q"], level["d"]
         other = lax.rem(slot + 1, SLOTS)
         half_round(level, slot, a, b, True)
-        arrived(q, d, other, False)
-        correct(level, slot, other, b)
+        arrived_corners(slot)
+        arrived_cross(q, other)
+        arrived_slab(q, d, other)
+
+        def add_slab(k, at, part):
+            hx[other, k, at, :] = hx[other, k, at, :] + part
+
+        def add_cross(m, at, part):
+            hy[other, m, at, :] = hy[other, m, at, :] + part
+
+        correct(level, slot, b, add_slab, add_cross)
         sent(q, d, slot, True)
 
-    def lift_faces(qc, qf, slot):
+    def lift_slab(qc, qf, slot):
+        table = lagrange(qf, qc)
+        for k in range(2):
+            lines_in = tiles(hx[slot, k, pl.ds(0, qc * qc * NY), :], qc, qc)
+            for j in range(qf):
+                line = weighted(table[j], [lines_in[n] for n in range(qc)])
+                for n in range(qf):
+                    hxl[k, pl.ds((j * qf + n) * NY, NY), :] = weighted(table[n], [line[e] for e in range(qc)])
+
+    def lift_cross(qc, qf, slot):
         table = lagrange(qf, qc)
         spread = []
         for e in range(qc):
@@ -582,11 +652,6 @@
                     column = jnp.where(row == n, float(table[n, e]), column)
             spread.append(column)
         for k in range(2):
-            lines_in = tiles(hx[slot, k, pl.ds(0, qc * qc * NY), :], qc, qc)
-            for j in range(qf):
-                line = weighted(table[j], [lines_in[n] for n in range(qc)])
-                for n in range(qf):
-                    hxl[k, pl.ds((j * qf + n) * NY, NY), :] = weighted(table[n], [line[e] for e in range(qc)])
             for i in range(qf):
                 line = weighted(table[i], [hy[slot, k, pl.ds(a * NY, qc), :] for a in range(qc)])
                 value = spread[0] * line[0:1]
@@ -599,9 +664,6 @@
         following = (here + 1) % SLOTS
         prolong(coarse["d"].at[slot], d, here, x, q, coarse["q"])
         local_part(level, here)
-        if awaited:
-            arrived(coarse["q"], coarse["d"], slot, False)
-        lift_faces(coarse["q"], q, slot)
 
         def put(at, part):
             r[at, :] = r[at, :] + part
@@ -611,10 +673,23 @@
             d[following, at, :] = value
             x[at, :] = x[at, :] + value
 
+        if awaited:
+            arrived_cross(coarse["q"], slot)
+        lift_cross(coarse["q"], q, slot)
         rims(level, hyl, put)
-        for k in range(2):
-            put(face_at(k, q, 0, q), slab_term(level, hxl, k, 0, q))
-        planes(q, advance)
+
+        def inside(i, carry):
+            advance(plane_at(i, q))
+            return carry
+
+        lax.fori_loop(1, q - 1, inside, 0)
+        if awaited:
+            arrived_slab(coarse["q"], coarse["d"], slot)
+        lift_slab(coarse["q"], q, slot)
+        for k in range(2):
+            at = face_at(k, q, 0, q)
+            put(at, slab_term(level, hxl, k, 0, q))
+            advance(at)
         send_all(q, d, following, with_corners)
         if awaited:
             sent(coarse["q"], coarse["d"], slot, False)
@@ -631,6 +706,72 @@
 
         lax.fori_loop(0, q, body, 0)
         send_all(q, d, slot, with_corners)
+
+    def opening_step(level, factor, a, b):
+        q, d, r, x, inv = (level[name] for name in ("q", "d", "r", "x", "inv"))
+        p = PENALTY[q]
+
+        def start(at):
+            value = inv[at, :] * r[at, :] * factor
+            d[0, at, :] = value
+            x[at, :] = value
+
+        def put(at, part):
+            r[at, :] = r[at, :] + part
+
+        def advance(at):
+            value = a * d[0, at, :] + b * inv[at, :] * r[at, :]
+            d[1, at, :] = value
+            x[at, :] = x[at, :] + value
+
+        planes(q, start)
+        slab_do(far, "wait_send", q, raw, 0, None, False)
+        slab_do(near, "wait_send", q, raw, 0, None, False)
+        local_part(level, 0)
+        coefs_done(range(4, 8))
+        for k in range(2):
+            own = hc[k, 0]
+            y_pair = cross_weights(own, hcc[2 * k], hcc[2 * k + 1])
+            z_pair = end_weights(own, hc[k, 1])
+            y_pair, z_pair = ([jnp.broadcast_to(p * w, (q, NY, NZ)) for w in pair] for pair in (y_pair, z_pair))
+            base = ends_added(tiles(gx5[k], q, q) * own + p * weights[k], q, y_pair, z_pair)
+            gx5[k] = (1.0 / base).reshape(q * q * NY, NZ)
+        node = lax.broadcasted_iota(jnp.int32, (q, NZ), 0)
+        for m in range(2):
+            here, theirs = m * (NY - 1), (1 - m) * (NY - 1)
+            low, high = (w[theirs : theirs + 1] for w in end_weights(hc[2 + m, 0], hc[2 + m, 1]))
+            own = hc[2 + m, 0, pl.ds(theirs, 1), :]
+            across = p * weights[2 + m, pl.ds(here, 1), :]
+            along = p * (jnp.where(node == 0, low, 0.0) + jnp.where(node == q - 1, high, 0.0))
+            for i in range(q):
+                at = pl.ds(i * NY, q)
+                base = gy5[m, at, :] * own + across + along
+                for k in range(2):
+                    if i == k * (q - 1):
+                        base = base + p * (0.5 * (own + hcc[2 * k + m, pl.ds(theirs, 1), :]))
+                gy5[m, at, :] = 1.0 / base
+        for k in range(2):
+            cross_do(k, "wait_recv", q, 0, True)
+        for m in range(2):
+            for i in range(q):
+                at = pl.ds(i * NY, q)
+                hy[0, m, at, :] = gy5[m, at, :] * hy[0, m, at, :] * factor
+        rims(level, hy.at[0], put)
+
+        def inside(i, carry):
+            advance(plane_at(i, q))
+            return carry
+
+        lax.fori_loop(1, q - 1, inside, 0)
+        for k in (near, far):
+            slab_do(k, "wait_recv", q, raw, 0, None, True)
+            hx[0, k] = gx5[k] * hx[0, k] * factor
+            at = face_at(k, q, 0, q)
+            put(at, slab_term(level, hx.at[0], k, 0, q))
+            advance(at)
+        send_all(q, d, 1, False)
+        for k in range(2):
+            cross_do(k, "wait_send", q, 0, False)
 
     def pick(k, values):
         out = jnp.float32(values[0])
@@ -710,8 +851,8 @@
 
     first, pairs = chebyshev_factors(DEGREE, LAMBDA_TOP / 8.0)
     coarse_first, coarse_pairs = chebyshev_factors(COARSE_ITERS, LAMBDA_TOP / 40.0)
-    first_update(five, 0, first, False)
-    run(five, 0, pairs, True)
+    opening_step(five, first, *pairs[0])
+    run(five, 1, pairs[1:], True)
     restrict(res, r3, Q5, Q3)
     first_update(three, 3, first, True)
     greeted()
@@ -731,6 +872,18 @@
     double_step(three, 14 % SLOTS, *pairs, False, True)
     lifted_step(three, 16 % SLOTS, five, 16 % SLOTS, first, True, False)
     run(five, 17, pairs, True)
+
+
+def hand_out(sol, res, sol_out, res_out, done):
+    rows = Q5**3 * NY // 4
+    copies = [
+        pltpu.make_async_copy(src.at[pl.ds(n * rows, rows), :], dst.at[pl.ds(n * rows, rows), :], done.at[k, n])
+        for k, (src, dst) in enumerate(((sol, sol_out), (res, res_out))) for n in range(4)
+    ]
+    for copy in copies:
+        copy.start()
+    for copy in copies:
+        copy.wait()
 
 
 def per_device(right_side, coefficient, bottom_top, stiff_five, stiff_three, stiff_one):
@@ -748,7 +901,7 @@
         in_specs=[hbm] * 6,
         out_specs=[vmem, vmem],
         scratch_shapes=[
-            field(NY), pltpu.SMEM((2, NY), jnp.int32), pltpu.VMEM((Q5**3, Q5**3), F32), pltpu.VMEM((Q3**3, Q3**3), F32),
+            two(NY), pltpu.SMEM((2, NY), jnp.int32), pltpu.VMEM((Q5**3, Q5**3), F32), pltpu.VMEM((Q3**3, Q3**3), F32),
             pltpu.SMEM((Q1**3, Q1**3), F32),
             slots(n5), field(n5), field(n5),
             field(n3), field(n3), slots(n3), field(n3), field(n3),
@@ -756,12 +909,13 @@
             pltpu.VMEM((224, 224), BF16), pltpu.VMEM((224, 224), BF16),
             pltpu.VMEM((64, 64), BF16), pltpu.VMEM((64, 64), BF16),
             field(6 * 16 * NY), pltpu.VMEM((6, NY, NZ), F32),
-            slots(2, Q5 * Q5 * NY), slots(2, Q5 * NY), two(Q5 * Q5 * NY), slots(2, Q5 * NY), pltpu.VMEM((4, NY, NZ), F32),
+            slots(2, Q5 * Q5 * NY), slots(2, Q5 * NY), two(Q5 * Q5 * NY), slots(2, Q5 * NY), pltpu.VMEM((4, 2, NY, NZ), F32),
             slots(4, NY), slots(4, NY), two(Q3 * NY),
             two(Q3 * Q3 * NY), two(Q1 * Q1 * NY), two(Q3 * NY), two(Q1 * NY), two(Q3 * NY), two(Q1 * NY),
             pltpu.VMEM((4, 2, NY, NZ), F32), two(Q5 * Q5 * NY), two(Q5 * NY),
+            pltpu.VMEM((4, NY, NZ), F32), two(Q5 * Q5 * NY), two(Q5 * NY),
             dma((2, 4, SLOTS)), dma((2, 4, SLOTS)), dma((2, SLOTS)), dma((2, SLOTS)), dma((4, SLOTS)), dma((4, SLOTS)),
-            dma((4, 3)), dma((4, 3)), dma((4,)), dma((4,)), dma((6,)),
+            dma((4, 3)), dma((4, 3)), dma((8,)), dma((8,)), dma((6,)),
         ],
         compiler_params=pltpu.CompilerParams(
             collective_id=0, has_side_effects=True, vmem_limit_bytes=48 * 2**20
@@ -775,6 +929,13 @@
             )
         )
     )
+    sol, res = pl.pallas_call(
+        hand_out,
+        out_shape=[jax.ShapeDtypeStruct((n5, NZ), F32)] * 2,
+        in_specs=[vmem] * 2,
+        out_specs=[hbm, hbm],
+        scratch_shapes=[dma((2, 4))],
+    )(*(pltpu.with_memory_space_constraint(value, pltpu.VMEM) for value in (sol, res)))
     return sol.reshape(shape), res.reshape(shape)
 
 

time: 86.6 us -> 81.8 us (0.945); the launches traced: 85.4 us -> 81.7 us
  local copies, waits for them, and re-layouts: 1.83 us -> 0 us
  Pallas kernels: 82.9 us -> 81.1 us
    pallas_call x1, Pallas kernels: 82.9 us -> 79.8 us  [per_device(): pl.pallas_call(kernel, out_shape=[jax.ShapeDtypeStruct((n5, NZ), F32)] *...]
    unnamed x2 -> x0, local copies, waits for them, and re-layouts: 1.83 us -> none
    pallas_call x0 -> x1, Pallas kernels: none -> 1.27 us  [per_device(): pl.pallas_call(hand_out, out_shape=[jax.ShapeDtypeStruct((n5, NZ), F32)]...]
where the time goes in v4:
time: 81.8 us; the launch traced here: 81.7 us
  Pallas kernels  81.1 us (99%)
    pallas_call x1, Pallas kernels, per_device(): pl.pallas_call(kernel, out_shape=[jax.ShapeDtypeStruct((n5, NZ), F32)] *...  79.8 us

profile of v4, /device:TPU:13, one launch (start us, length us, event | category | flops | bytes accessed | tf_op | source)
XLA Modules:
  0.0 81.7 jit_solution(12211402305084513767)
XLA Ops:
  0.6 79.8 %shard_map.77 = (f32[1728,128]{1,0:T(8,128)S(1)}, f32[1728,128]{1,0:T(8,128)S(1)}) custom-call(f32[8,128]{1,0:T(8,128)} %bitcast.10, s32[2,8]{1,0:T(2,128)} %bitcast.11, f32[1728,128]{1,0:T(8,128)} %bitcast.9, f32[216,216]{1,0:T(8,128)} %s5_in.1, f32[64,64]{1,0:T(8,128)} %s3_in.1, f32[8,8]{1,0:T(8,128)} %s1_in.1), custom_call_target="tpu_custom_call" | custom-call | tf_op jit(solution)/shard_map/pallas_call | solution.py:898
  80.4 1.3 %shard_map.78 = (f32[1728,128]{1,0:T(8,128)}, f32[1728,128]{1,0:T(8,128)}) custom-call(f32[1728,128]{1,0:T(8,128)S(1)} %get-tuple-element.6.sol, f32[1728,128]{1,0:T(8,128)S(1)} %get-tuple-element.7.res), custom_call_target="tpu_custom_call" | custom-call | tf_op jit(solution)/shard_map/pallas_call | solution.py:932

commit v5 on v4

--- a/solution.py
+++ b/solution.py
@@ -475,7 +475,7 @@
         part = PENALTY[q] * weights[k] * tiles(source[k, pl.ds(first * q * NY, count * q * NY), :], count * q)
         return part.reshape(count * q * NY, NZ)
 
-    def step(level, slot, a, b, update, send):
+    def step(level, slot, a, b, update, send, settled=False):
         q, d, r, x, inv = (level[name] for name in ("q", "d", "r", "x", "inv"))
         other = lax.rem(slot + 1, SLOTS)
 
@@ -520,9 +520,10 @@
                 if number == 0:
                     send_cross(q, d, other)
                 send_far(q, d, other, group)
-        sent(q, d, slot, False)
-
-    def correct(level, slot, b, slab_put, cross_put):
+        if not settled:
+            sent(q, d, slot, False)
+
+    def correct(level, slot, rows, b, slab_put, cross_put):
         q, d, gx, gy = (level[name] for name in ("q", "d", "gx", "gy"))
         p = PENALTY[q]
         face = q * q * NY
@@ -536,10 +537,10 @@
             at = pl.ds(0, face)
             slab_put(k, at, b * gx[k, at, :] * term.reshape(face, NZ))
         for m in range(2):
-            mine, theirs = pl.ds(m * (NY - 1), 1), pl.ds((1 - m) * (NY - 1), 1)
+            here, theirs = pl.ds(m * (NY - 1), 1), pl.ds((1 - m) * (NY - 1), 1)
             for i in range(q):
                 at = pl.ds(i * NY, q)
-                term = p * weights[2 + m, mine, :] * pack[slot, m, at, :]
+                term = p * weights[2 + m, here, :] * rows[m, at, :]
                 for k in range(2):
                     if i == k * (q - 1):
                         term = term + p * gw[2 + m, k, theirs, :] * hd[slot, 2 * k + m, pl.ds(0, q), :]
@@ -574,6 +575,12 @@
         for k in range(2):
             put_both(face_at(k, q, 0, q), slab_term(level, hx.at[slot], k, 0, q))
 
+    def keep_slab(k, at, part):
+        hxl[k, at, :] = part
+
+    def keep_cross(m, at, part):
+        hyl[m, at, :] = part
+
     def double_step(level, slot, first, second, with_corners, total):
         q, d, r, x, inv = (level[name] for name in ("q", "d", "r", "x", "inv"))
         other, third = lax.rem(slot + 1, SLOTS), lax.rem(slot + 2, SLOTS)
@@ -597,13 +604,7 @@
         local_part(level, other)
         arrived_corners(slot)
 
-        def keep_slab(k, at, part):
-            hxl[k, at, :] = part
-
-        def keep_cross(m, at, part):
-            hyl[m, at, :] = part
-
-        correct(level, slot, first[1], keep_slab, keep_cross)
+        correct(level, slot, pack.at[slot], first[1], keep_slab, keep_cross)
         rims(level, hyl, put)
         for k in range(2):
             put(face_at(k, q, 0, q), slab_term(level, hxl, k, 0, q))
@@ -630,7 +631,7 @@
         def add_cross(m, at, part):
             hy[other, m, at, :] = hy[other, m, at, :] + part
 
-        correct(level, slot, b, add_slab, add_cross)
+        correct(level, slot, pack.at[slot], b, add_slab, add_cross)
         sent(q, d, slot, True)
 
     def lift_slab(qc, qf, slot):
@@ -642,7 +643,7 @@
                 for n in range(qf):
                     hxl[k, pl.ds((j * qf + n) * NY, NY), :] = weighted(table[n], [line[e] for e in range(qc)])
 
-    def lift_cross(qc, qf, slot):
+    def spread_table(qc, qf):
         table = lagrange(qf, qc)
         spread = []
         for e in range(qc):
@@ -651,19 +652,33 @@
                 if table[n, e] != 0.0:
                     column = jnp.where(row == n, float(table[n, e]), column)
             spread.append(column)
+        return spread
+
+    def lift_line(spread, line):
+        value = spread[0] * line[0:1]
+        for e in range(1, len(spread)):
+            value = value + spread[e] * line[e : e + 1]
+        return value
+
+    def lift_cross(qc, qf, slot):
+        table, spread = lagrange(qf, qc), spread_table(qc, qf)
         for k in range(2):
             for i in range(qf):
                 line = weighted(table[i], [hy[slot, k, pl.ds(a * NY, qc), :] for a in range(qc)])
-                value = spread[0] * line[0:1]
-                for e in range(1, qc):
-                    value = value + spread[e] * line[e : e + 1]
-                hyl[k, pl.ds(i * NY, NY), :] = value
-
-    def lifted_step(coarse, slot, level, here, factor, awaited, with_corners):
+                hyl[k, pl.ds(i * NY, NY), :] = lift_line(spread, line)
+
+    def lift_corners(qc, qf, slot):
+        spread = spread_table(qc, qf)
+        for g in range(4):
+            hd[slot, g] = lift_line(spread, hd[slot, g])
+
+    def lifted_step(coarse, slot, level, here, factor):
         q, d, r, x, inv = (level[name] for name in ("q", "d", "r", "x", "inv"))
         following = (here + 1) % SLOTS
         prolong(coarse["d"].at[slot], d, here, x, q, coarse["q"])
         local_part(level, here)
+        lift_cross(coarse["q"], q, slot)
+        lift_slab(coarse["q"], q, slot)
 
         def put(at, part):
             r[at, :] = r[at, :] + part
@@ -673,26 +688,50 @@
             d[following, at, :] = value
             x[at, :] = x[at, :] + value
 
-        if awaited:
-            arrived_cross(coarse["q"], slot)
-        lift_cross(coarse["q"], q, slot)
         rims(level, hyl, put)
-
-        def inside(i, carry):
-            advance(plane_at(i, q))
-            return carry
-
-        lax.fori_loop(1, q - 1, inside, 0)
-        if awaited:
-            arrived_slab(coarse["q"], coarse["d"], slot)
-        lift_slab(coarse["q"], q, slot)
-        for k in range(2):
-            at = face_at(k, q, 0, q)
-            put(at, slab_term(level, hxl, k, 0, q))
-            advance(at)
-        send_all(q, d, following, with_corners)
-        if awaited:
-            sent(coarse["q"], coarse["d"], slot, False)
+        for k in range(2):
+            put(face_at(k, q, 0, q), slab_term(level, hxl, k, 0, q))
+        planes(q, advance)
+        send_all(q, d, following, True)
+
+    def lifted_round(coarse, level, here, factor):
+        q, d, r, x, inv = (level[name] for name in ("q", "d", "r", "x", "inv"))
+        qc, other, spare = coarse["q"], (here + 1) % SLOTS, (here + 3) % SLOTS
+
+        def partial_next(at):
+            d[other, at, :] = factor * inv[at, :] * r[at, :]
+
+        def put(at, part):
+            r[at, :] = r[at, :] + part
+
+        def put_both(at, part):
+            r[at, :] = r[at, :] + part
+            d[other, at, :] = d[other, at, :] + factor * inv[at, :] * part
+
+        def add(at):
+            x[at, :] = x[at, :] + d[other, at, :]
+
+        prolong(coarse["d"].at[here], d, here, x, q, qc)
+        local_part(level, here)
+        planes(q, partial_next)
+        send_all(q, d, other, False)
+        pack_rows(q, d.at[here], pack.at[spare])
+        arrived_cross(qc, here)
+        lift_cross(qc, q, here)
+        arrived_slab(qc, coarse["d"], here)
+        lift_slab(qc, q, here)
+        sent(q, d, other, False)
+        rims(level, hyl, put_both)
+        for k in range(2):
+            put_both(face_at(k, q, 0, q), slab_term(level, hxl, k, 0, q))
+        planes(q, add)
+        arrived_corners(here)
+        lift_corners(qc, q, here)
+        correct(level, here, pack.at[spare], factor, keep_slab, keep_cross)
+        rims(level, hyl, put)
+        for k in range(2):
+            put(face_at(k, q, 0, q), slab_term(level, hxl, k, 0, q))
+        sent(qc, coarse["d"], here, True)
 
     def first_update(level, slot, factor, with_corners):
         q, d, x, r, inv = (level[name] for name in ("q", "d", "x", "r", "inv"))
@@ -773,6 +812,14 @@
         for k in range(2):
             cross_do(k, "wait_send", q, 0, False)
 
+            @pl.when(jnp.logical_not(sides[k][2]))
+            def _(k=k):
+                gx5[k] = jnp.zeros_like(gx5[k])
+
+            @pl.when(jnp.logical_not(sides[2 + k][2]))
+            def _(k=k):
+                gy5[k] = jnp.zeros_like(gy5[k])
+
     def pick(k, values):
         out = jnp.float32(values[0])
         for n in range(1, len(values)):
@@ -845,7 +892,7 @@
 
         lax.fori_loop(0, qf, body, 0)
 
-    five = dict(q=Q5, d=d5, t=t5, r=res, x=sol, inv=inv5, product=lambda slot: product_wide(Q5, d5, slot, t5, sh5, sl5))
+    five = dict(q=Q5, d=d5, t=t5, r=res, x=sol, inv=inv5, gx=gx5, gy=gy5, product=lambda slot: product_wide(Q5, d5, slot, t5, sh5, sl5))
     three = dict(q=Q3, d=d3, t=t3, r=r3, x=x3, inv=inv3, gx=gx3, gy=gy3, product=lambda slot: product_wide(Q3, d3, slot, t3, sh3, sl3))
     one = dict(q=Q1, d=d1, t=t1, r=r1, x=x1, inv=inv1, gx=gx1, gy=gy1, product=lambda slot: product_small(d1, slot, t1))
 
@@ -868,10 +915,11 @@
 
     lax.fori_loop(0, 3, coarse_rounds, 0)
     finish_round(one, 12 % SLOTS, *coarse_pairs[6])
-    lifted_step(one, 13 % SLOTS, three, 13 % SLOTS, first, False, True)
-    double_step(three, 14 % SLOTS, *pairs, False, True)
-    lifted_step(three, 16 % SLOTS, five, 16 % SLOTS, first, True, False)
-    run(five, 17, pairs, True)
+    lifted_step(one, 13 % SLOTS, three, 13 % SLOTS, first)
+    double_step(three, 14 % SLOTS, *pairs, True, True)
+    lifted_round(three, five, 16 % SLOTS, first)
+    step(five, 17 % SLOTS, *pairs[0], True, True, settled=True)
+    run(five, 18, pairs[1:], True)
 
 
 def hand_out(sol, res, sol_out, res_out, done):
@@ -910,7 +958,7 @@
             pltpu.VMEM((64, 64), BF16), pltpu.VMEM((64, 64), BF16),
             field(6 * 16 * NY), pltpu.VMEM((6, NY, NZ), F32),
             slots(2, Q5 * Q5 * NY), slots(2, Q5 * NY), two(Q5 * Q5 * NY), slots(2, Q5 * NY), pltpu.VMEM((4, 2, NY, NZ), F32),
-            slots(4, NY), slots(4, NY), two(Q3 * NY),
+            slots(4, NY), slots(4, NY), two(Q5 * NY),
             two(Q3 * Q3 * NY), two(Q1 * Q1 * NY), two(Q3 * NY), two(Q1 * NY), two(Q3 * NY), two(Q1 * NY),
             pltpu.VMEM((4, 2, NY, NZ), F32), two(Q5 * Q5 * NY), two(Q5 * NY),
             pltpu.VMEM((4, NY, NZ), F32), two(Q5 * Q5 * NY), two(Q5 * NY),

time: 81.8 us -> 80.3 us (0.982)
  the two profiles are of different devices: /device:TPU:13 before, /device:TPU:11 now
where the time goes in v5:
time: 80.3 us; the launch traced here: 80.1 us
  Pallas kernels  79.5 us (99%)
    pallas_call x1, Pallas kernels, per_device(): pl.pallas_call(kernel, out_shape=[jax.ShapeDtypeStruct((n5, NZ), F32)] *...  78.2 us

profile of v5, /device:TPU:11, one launch (start us, length us, event | category | flops | bytes accessed | tf_op | source)
XLA Modules:
  0.0 80.1 jit_solution(1246140405762116787)
XLA Ops:
  0.6 78.2 %shard_map.77 = (f32[1728,128]{1,0:T(8,128)S(1)}, f32[1728,128]{1,0:T(8,128)S(1)}) custom-call(f32[8,128]{1,0:T(8,128)} %bitcast.10, s32[2,8]{1,0:T(2,128)} %bitcast.11, f32[1728,128]{1,0:T(8,128)} %bitcast.9, f32[216,216]{1,0:T(8,128)} %s5_in.1, f32[64,64]{1,0:T(8,128)} %s3_in.1, f32[8,8]{1,0:T(8,128)} %s1_in.1), custom_call_target="tpu_custom_call" | custom-call | tf_op jit(solution)/shard_map/pallas_call | solution.py:946
  78.8 1.3 %shard_map.78 = (f32[1728,128]{1,0:T(8,128)}, f32[1728,128]{1,0:T(8,128)}) custom-call(f32[1728,128]{1,0:T(8,128)S(1)} %get-tuple-element.6.sol, f32[1728,128]{1,0:T(8,128)S(1)} %get-tuple-element.7.res), custom_call_target="tpu_custom_call" | custom-call | tf_op jit(solution)/shard_map/pallas_call | solution.py:980

commit v6 on v5

--- a/solution.py
+++ b/solution.py
@@ -149,6 +149,10 @@
             return [(0, q)]
         return [(0, 1), (q - 1, 1)] + [(j, min(2, q - 1 - j)) for j in range(1, q - 1, 2)]
 
+    def groups(q):
+        count = len(lines(q))
+        return [[0, 1]] + [[n] for n in range(2, count)] if count > 1 else [[0]]
+
     def face_at(k, q, first, count):
         return pl.ds(pl.multiple_of(k * ((q**3 - q * q) * NY) + first * q * NY, NY), count * q * NY)
 
@@ -222,8 +226,8 @@
         if with_corners:
             send_corners(q, d, slot)
         send_cross(q, d, slot)
+        send_near(q, d, slot)
         send_far(q, d, slot, range(len(lines(q))))
-        send_near(q, d, slot)
 
     def arrived_cross(q, slot):
         for k in range(2):
@@ -277,8 +281,8 @@
     raw = Unslotted(res)
     for k in range(2):
         cross_do(k, "start", Q5, 0, False)
-    slab_do(far, "start", Q5, raw, 0, None, False)
-    slab_do(near, "start", Q5, raw, 0, None, False)
+    send_near(Q5, raw, 0)
+    send_far(Q5, raw, 0, range(len(lines(Q5))))
 
     def split(table, high, low, count):
         value = table[...]
@@ -361,44 +365,7 @@
 
         lax.fori_loop(0, q, body, 0)
 
-    invert(Q3, inv3)
-    invert(Q1, inv1)
-
-    pack_rows(Q3, inv3, gp3)
-    pack_rows(Q1, inv1, gp1)
-
-    def greet_copy(k, n, arriving):
-        here = k if arriving else k ^ 1
-        if n == 0:
-            src, dst = weights.at[pl.ds(2 if k < 2 else 0, 2)], gw.at[here]
-        elif k < 2:
-            q, inv, target = ((Q3, inv3, gx3), (Q1, inv1, gx1))[n - 1]
-            src, dst = inv.at[pl.ds(k * (q**3 - q * q) * NY, q * q * NY), :], target.at[here]
-        else:
-            source, target = ((gp3, gy3), (gp1, gy1))[n - 1]
-            src, dst = source.at[k - 2], target.at[here - 2]
-        return pltpu.make_async_remote_copy(
-            src_ref=src, dst_ref=dst, send_sem=gs.at[k, n], recv_sem=gr.at[here, n],
-            device_id={sides[k][0]: sides[k][1]}, device_id_type=MESH,
-        )
-
-    for k in (2, 3, 0, 1):
-
-        @pl.when(sides[k][2])
-        def _(k=k):
-            for n in range(3):
-                greet_copy(k, n, False).start()
-
     invert(Q5, inv5)
-
-    def greeted():
-        for k in range(4):
-
-            @pl.when(sides[k][2])
-            def _(k=k):
-                for n in range(3):
-                    greet_copy(k, n, True).wait_recv()
-                    greet_copy(k, n, False).wait_send()
 
     def product_wide(q, d, slot, t, high, low):
         count = q**3
@@ -475,7 +442,7 @@
         part = PENALTY[q] * weights[k] * tiles(source[k, pl.ds(first * q * NY, count * q * NY), :], count * q)
         return part.reshape(count * q * NY, NZ)
 
-    def step(level, slot, a, b, update, send, settled=False):
+    def step(level, slot, a, b, update, send, settled=False, meanwhile=None):
         q, d, r, x, inv = (level[name] for name in ("q", "d", "r", "x", "inv"))
         other = lax.rem(slot + 1, SLOTS)
 
@@ -510,12 +477,12 @@
         slab_face(near, 0, q)
         if send:
             send_near(q, d, other)
-        pieces = lines(q)
-        groups = [[0, 1]] + [[n] for n in range(2, len(pieces))] if len(pieces) > 1 else [[0]]
-        for number, group in enumerate(groups):
+        if meanwhile is not None:
+            meanwhile()
+        for number, group in enumerate(groups(q)):
             for piece in group:
                 slab_do(far, "wait_recv", q, d, slot, piece, True)
-                slab_face(far, *pieces[piece])
+                slab_face(far, *lines(q)[piece])
             if send:
                 if number == 0:
                     send_cross(q, d, other)
@@ -764,8 +731,9 @@
             x[at, :] = x[at, :] + value
 
         planes(q, start)
-        slab_do(far, "wait_send", q, raw, 0, None, False)
         slab_do(near, "wait_send", q, raw, 0, None, False)
+        for piece in range(len(lines(q))):
+            slab_do(far, "wait_send", q, raw, 0, piece, False)
         local_part(level, 0)
         coefs_done(range(4, 8))
         for k in range(2):
@@ -802,13 +770,24 @@
             return carry
 
         lax.fori_loop(1, q - 1, inside, 0)
-        for k in (near, far):
-            slab_do(k, "wait_recv", q, raw, 0, None, True)
-            hx[0, k] = gx5[k] * hx[0, k] * factor
-            at = face_at(k, q, 0, q)
-            put(at, slab_term(level, hx.at[0], k, 0, q))
+
+        def slab_face(k, first, count):
+            inside_face = pl.ds(first * q * NY, count * q * NY)
+            hx[0, k, inside_face, :] = gx5[k, inside_face, :] * hx[0, k, inside_face, :] * factor
+            at = face_at(k, q, first, count)
+            put(at, slab_term(level, hx.at[0], k, first, count))
             advance(at)
-        send_all(q, d, 1, False)
+
+        slab_do(near, "wait_recv", q, raw, 0, None, True)
+        slab_face(near, 0, q)
+        send_near(q, d, 1)
+        for number, group in enumerate(groups(q)):
+            for piece in group:
+                slab_do(far, "wait_recv", q, raw, 0, piece, True)
+                slab_face(far, *lines(q)[piece])
+            if number == 0:
+                send_cross(q, d, 1)
+            send_far(q, d, 1, group)
         for k in range(2):
             cross_do(k, "wait_send", q, 0, False)
 
@@ -826,7 +805,7 @@
             out = jnp.where(k == n, jnp.float32(values[n]), out)
         return out
 
-    def run(level, exchange, factors, last):
+    def run(level, exchange, factors, last, meanwhile=None):
         loop = len(factors) if last else len(factors) - 1
 
         def body(k, carry):
@@ -837,7 +816,7 @@
         lax.fori_loop(0, loop, body, 0)
         slot = (exchange + loop) % SLOTS
         if last:
-            step(level, slot, 0.0, 0.0, False, False)
+            step(level, slot, 0.0, 0.0, False, False, meanwhile=meanwhile)
         else:
             step(level, slot, *factors[-1], True, False)
 
@@ -863,6 +842,17 @@
             return carry
 
         lax.fori_loop(0, qc, gather, 0)
+
+    def restrict_face(slot, k, coarse, qf, qc):
+        table = lagrange(qf, qc)
+        lines_in = tiles(hx[slot, k, pl.ds(0, qf * qf * NY), :], qf, qf)
+        weight = PENALTY[qf] * weights[k]
+        for b in range(qc):
+            line = weighted(table[:, b], [lines_in[j] for j in range(qf)])
+            for e in range(qc):
+                value = weight * weighted(table[:, e], [line[n] for n in range(qf)])
+                at = pl.ds(pl.multiple_of(k * ((qc**3 - qc * qc) * NY) + (b * qc + e) * NY, NY), NY)
+                coarse[at, :] = coarse[at, :] + value
 
     def prolong(coarse, fine, slot, sum_into, qf, qc):
         table = lagrange(qf, qc)
@@ -898,9 +888,47 @@
 
     first, pairs = chebyshev_factors(DEGREE, LAMBDA_TOP / 8.0)
     coarse_first, coarse_pairs = chebyshev_factors(COARSE_ITERS, LAMBDA_TOP / 40.0)
+    invert(Q3, inv3)
+    invert(Q1, inv1)
+
+    pack_rows(Q3, inv3, gp3)
+    pack_rows(Q1, inv1, gp1)
+
+    def greet_copy(k, n, arriving):
+        here = k if arriving else k ^ 1
+        if n == 0:
+            src, dst = weights.at[pl.ds(2 if k < 2 else 0, 2)], gw.at[here]
+        elif k < 2:
+            q, inv, target = ((Q3, inv3, gx3), (Q1, inv1, gx1))[n - 1]
+            src, dst = inv.at[pl.ds(k * (q**3 - q * q) * NY, q * q * NY), :], target.at[here]
+        else:
+            source, target = ((gp3, gy3), (gp1, gy1))[n - 1]
+            src, dst = source.at[k - 2], target.at[here - 2]
+        return pltpu.make_async_remote_copy(
+            src_ref=src, dst_ref=dst, send_sem=gs.at[k, n], recv_sem=gr.at[here, n],
+            device_id={sides[k][0]: sides[k][1]}, device_id_type=MESH,
+        )
+
+    for k in (2, 3, 0, 1):
+
+        @pl.when(sides[k][2])
+        def _(k=k):
+            for n in range(3):
+                greet_copy(k, n, False).start()
+
     opening_step(five, first, *pairs[0])
-    run(five, 1, pairs[1:], True)
-    restrict(res, r3, Q5, Q3)
+
+    def greeted():
+        for k in range(4):
+
+            @pl.when(sides[k][2])
+            def _(k=k):
+                for n in range(3):
+                    greet_copy(k, n, True).wait_recv()
+                    greet_copy(k, n, False).wait_send()
+
+    run(five, 1, pairs[1:], True, lambda: restrict(res, r3, Q5, Q3))
+    restrict_face(2, far, r3, Q5, Q3)
     first_update(three, 3, first, True)
     greeted()
     double_step(three, 3, *pairs, False, False)

time: 80.3 us -> 79.1 us (0.985)
  the two profiles are of different devices: /device:TPU:11 before, /device:TPU:13 now
where the time goes in v6:
time: 79.1 us; the launch traced here: 78.1 us
  Pallas kernels  77.4 us (98%)
    pallas_call x1, Pallas kernels, per_device(): pl.pallas_call(kernel, out_shape=[jax.ShapeDtypeStruct((n5, NZ), F32)] *...  76.2 us

profile of v6, /device:TPU:13, one launch (start us, length us, event | category | flops | bytes accessed | tf_op | source)
XLA Modules:
  0.0 78.1 jit_solution(16299848872202185992)
XLA Ops:
  0.6 76.2 %shard_map.77 = (f32[1728,128]{1,0:T(8,128)S(1)}, f32[1728,128]{1,0:T(8,128)S(1)}) custom-call(f32[8,128]{1,0:T(8,128)} %bitcast.10, s32[2,8]{1,0:T(2,128)} %bitcast.11, f32[1728,128]{1,0:T(8,128)} %bitcast.9, f32[216,216]{1,0:T(8,128)} %s5_in.1, f32[64,64]{1,0:T(8,128)} %s3_in.1, f32[8,8]{1,0:T(8,128)} %s1_in.1), custom_call_target="tpu_custom_call" | custom-call | tf_op jit(solution)/shard_map/pallas_call | solution.py:974
  76.8 1.3 %shard_map.78 = (f32[1728,128]{1,0:T(8,128)}, f32[1728,128]{1,0:T(8,128)}) custom-call(f32[1728,128]{1,0:T(8,128)S(1)} %get-tuple-element.6.sol, f32[1728,128]{1,0:T(8,128)S(1)} %get-tuple-element.7.res), custom_call_target="tpu_custom_call" | custom-call | tf_op jit(solution)/shard_map/pallas_call | solution.py:1008

commit v7 on v6

--- a/solution.py
+++ b/solution.py
@@ -71,8 +71,8 @@
     mine, ends, s5, s3, s1,
     d5, t5, inv5, x3, r3, d3, t3, inv3, x1, r1, d1, t1, inv1,
     sh5, sl5, sh3, sl3, work, weights, hx, hy, ytile, pack, hc,
-    hd, dpack, dtile, gx3, gx1, gy3, gy1, gp3, gp1, gw, hxl, hyl, hcc, gx5, gy5,
-    xs, xr, ys, yr, cs, cr, gs, gr, csem, crsem, load,
+    hd, dpack, dtile, gx3, gx1, gy3, gy1, gw, hxl, hyl, hcc, gx5, gy5,
+    xs, xr, ys, yr, cs, cr, csem, crsem, load,
 ):
     slab, cross = lax.axis_index("slab"), lax.axis_index("cross")
     ns, nc = lax.axis_size("slab"), lax.axis_size("cross")
@@ -92,18 +92,12 @@
         @pl.when(jnp.logical_not(sides[k][2]))
         def _(k=k):
             hc[k] = jnp.zeros_like(hc[k])
-            gw[k] = jnp.zeros_like(gw[k])
-            gx3[k] = jnp.zeros_like(gx3[k])
-            gx1[k] = jnp.zeros_like(gx1[k])
             for slot in range(SLOTS):
                 hx[slot, k] = jnp.zeros_like(hx[slot, k])
 
         @pl.when(jnp.logical_not(sides[2 + k][2]))
         def _(k=k):
             hc[2 + k] = jnp.zeros_like(hc[2 + k])
-            gw[2 + k] = jnp.zeros_like(gw[2 + k])
-            gy3[k] = jnp.zeros_like(gy3[k])
-            gy1[k] = jnp.zeros_like(gy1[k])
             for slot in range(SLOTS):
                 hy[slot, k] = jnp.zeros_like(hy[slot, k])
 
@@ -307,11 +301,12 @@
     spread_diagonal(s3, inv3, Q3**3)
     for n in range(Q1**3):
         inv1[pl.ds(n * NY, NY), :] = jnp.full((NY, NZ), s1[n, n])
-    for k in range(2):
-        gx5[k] = inv5[face_at(1 - k, Q5, 0, Q5), :]
-        for i in range(Q5):
-            node = i * Q5 * Q5 + (1 - k) * Q5 * (Q5 - 1)
-            gy5[k, pl.ds(i * NY, Q5), :] = inv5[pl.ds(node * NY, Q5, stride=NY), :]
+    for q, inv, gx, gy in ((Q5, inv5, gx5, gy5), (Q3, inv3, gx3, gy3), (Q1, inv1, gx1, gy1)):
+        for k in range(2):
+            gx[k] = inv[face_at(1 - k, q, 0, q), :]
+            for i in range(q):
+                node = i * q * q + (1 - k) * q * (q - 1)
+                gy[k, pl.ds(i * NY, q), :] = inv[pl.ds(node * NY, q, stride=NY), :]
 
     def coefs_done(ks):
         for k in ks:
@@ -713,36 +708,15 @@
         lax.fori_loop(0, q, body, 0)
         send_all(q, d, slot, with_corners)
 
-    def opening_step(level, factor, a, b):
-        q, d, r, x, inv = (level[name] for name in ("q", "d", "r", "x", "inv"))
+    def neighbours_inverse(q, gx, gy):
         p = PENALTY[q]
-
-        def start(at):
-            value = inv[at, :] * r[at, :] * factor
-            d[0, at, :] = value
-            x[at, :] = value
-
-        def put(at, part):
-            r[at, :] = r[at, :] + part
-
-        def advance(at):
-            value = a * d[0, at, :] + b * inv[at, :] * r[at, :]
-            d[1, at, :] = value
-            x[at, :] = x[at, :] + value
-
-        planes(q, start)
-        slab_do(near, "wait_send", q, raw, 0, None, False)
-        for piece in range(len(lines(q))):
-            slab_do(far, "wait_send", q, raw, 0, piece, False)
-        local_part(level, 0)
-        coefs_done(range(4, 8))
         for k in range(2):
             own = hc[k, 0]
-            y_pair = cross_weights(own, hcc[2 * k], hcc[2 * k + 1])
-            z_pair = end_weights(own, hc[k, 1])
-            y_pair, z_pair = ([jnp.broadcast_to(p * w, (q, NY, NZ)) for w in pair] for pair in (y_pair, z_pair))
-            base = ends_added(tiles(gx5[k], q, q) * own + p * weights[k], q, y_pair, z_pair)
-            gx5[k] = (1.0 / base).reshape(q * q * NY, NZ)
+            y_pair, z_pair = (
+                [jnp.broadcast_to(p * w, (q, NY, NZ)) for w in pair] for pair in ((gw[k, 0], gw[k, 1]), end_weights(own, hc[k, 1]))
+            )
+            base = ends_added(tiles(gx[k], q, q) * own + p * weights[k], q, y_pair, z_pair)
+            gx[k] = (1.0 / base).reshape(q * q * NY, NZ)
         node = lax.broadcasted_iota(jnp.int32, (q, NZ), 0)
         for m in range(2):
             here, theirs = m * (NY - 1), (1 - m) * (NY - 1)
@@ -752,11 +726,51 @@
             along = p * (jnp.where(node == 0, low, 0.0) + jnp.where(node == q - 1, high, 0.0))
             for i in range(q):
                 at = pl.ds(i * NY, q)
-                base = gy5[m, at, :] * own + across + along
+                base = gy[m, at, :] * own + across + along
                 for k in range(2):
                     if i == k * (q - 1):
-                        base = base + p * (0.5 * (own + hcc[2 * k + m, pl.ds(theirs, 1), :]))
-                gy5[m, at, :] = 1.0 / base
+                        base = base + p * gw[2 + m, k, pl.ds(theirs, 1), :]
+                gy[m, at, :] = 1.0 / base
+
+    def zero_missing(gx, gy):
+        for k in range(2):
+
+            @pl.when(jnp.logical_not(sides[k][2]))
+            def _(k=k):
+                gx[k] = jnp.zeros_like(gx[k])
+
+            @pl.when(jnp.logical_not(sides[2 + k][2]))
+            def _(k=k):
+                gy[k] = jnp.zeros_like(gy[k])
+
+    def opening_step(level, factor, a, b):
+        q, d, r, x, inv = (level[name] for name in ("q", "d", "r", "x", "inv"))
+        p = PENALTY[q]
+
+        def start(at):
+            value = inv[at, :] * r[at, :] * factor
+            d[0, at, :] = value
+            x[at, :] = value
+
+        def put(at, part):
+            r[at, :] = r[at, :] + part
+
+        def advance(at):
+            value = a * d[0, at, :] + b * inv[at, :] * r[at, :]
+            d[1, at, :] = value
+            x[at, :] = x[at, :] + value
+
+        planes(q, start)
+        slab_do(near, "wait_send", q, raw, 0, None, False)
+        for piece in range(len(lines(q))):
+            slab_do(far, "wait_send", q, raw, 0, piece, False)
+        local_part(level, 0)
+        coefs_done(range(4, 8))
+        for k in range(2):
+            gw[k, 0], gw[k, 1] = cross_weights(hc[k, 0], hcc[2 * k], hcc[2 * k + 1])
+            for m in range(2):
+                gw[2 + m, k] = 0.5 * (hc[2 + m, 0] + hcc[2 * k + m])
+        neighbours_inverse(q, gx5, gy5)
         for k in range(2):
             cross_do(k, "wait_recv", q, 0, True)
         for m in range(2):
@@ -790,14 +804,7 @@
             send_far(q, d, 1, group)
         for k in range(2):
             cross_do(k, "wait_send", q, 0, False)
-
-            @pl.when(jnp.logical_not(sides[k][2]))
-            def _(k=k):
-                gx5[k] = jnp.zeros_like(gx5[k])
-
-            @pl.when(jnp.logical_not(sides[2 + k][2]))
-            def _(k=k):
-                gy5[k] = jnp.zeros_like(gy5[k])
+        zero_missing(gx5, gy5)
 
     def pick(k, values):
         out = jnp.float32(values[0])
@@ -805,7 +812,7 @@
             out = jnp.where(k == n, jnp.float32(values[n]), out)
         return out
 
-    def run(level, exchange, factors, last, meanwhile=None):
+    def run(level, exchange, factors, last):
         loop = len(factors) if last else len(factors) - 1
 
         def body(k, carry):
@@ -816,7 +823,7 @@
         lax.fori_loop(0, loop, body, 0)
         slot = (exchange + loop) % SLOTS
         if last:
-            step(level, slot, 0.0, 0.0, False, False, meanwhile=meanwhile)
+            step(level, slot, 0.0, 0.0, False, False)
         else:
             step(level, slot, *factors[-1], True, False)
 
@@ -888,49 +895,19 @@
 
     first, pairs = chebyshev_factors(DEGREE, LAMBDA_TOP / 8.0)
     coarse_first, coarse_pairs = chebyshev_factors(COARSE_ITERS, LAMBDA_TOP / 40.0)
-    invert(Q3, inv3)
-    invert(Q1, inv1)
-
-    pack_rows(Q3, inv3, gp3)
-    pack_rows(Q1, inv1, gp1)
-
-    def greet_copy(k, n, arriving):
-        here = k if arriving else k ^ 1
-        if n == 0:
-            src, dst = weights.at[pl.ds(2 if k < 2 else 0, 2)], gw.at[here]
-        elif k < 2:
-            q, inv, target = ((Q3, inv3, gx3), (Q1, inv1, gx1))[n - 1]
-            src, dst = inv.at[pl.ds(k * (q**3 - q * q) * NY, q * q * NY), :], target.at[here]
-        else:
-            source, target = ((gp3, gy3), (gp1, gy1))[n - 1]
-            src, dst = source.at[k - 2], target.at[here - 2]
-        return pltpu.make_async_remote_copy(
-            src_ref=src, dst_ref=dst, send_sem=gs.at[k, n], recv_sem=gr.at[here, n],
-            device_id={sides[k][0]: sides[k][1]}, device_id_type=MESH,
-        )
-
-    for k in (2, 3, 0, 1):
-
-        @pl.when(sides[k][2])
-        def _(k=k):
-            for n in range(3):
-                greet_copy(k, n, False).start()
-
     opening_step(five, first, *pairs[0])
 
-    def greeted():
-        for k in range(4):
-
-            @pl.when(sides[k][2])
-            def _(k=k):
-                for n in range(3):
-                    greet_copy(k, n, True).wait_recv()
-                    greet_copy(k, n, False).wait_send()
-
-    run(five, 1, pairs[1:], True, lambda: restrict(res, r3, Q5, Q3))
+    def prepare():
+        invert(Q3, inv3)
+        invert(Q1, inv1)
+        for q, gx, gy in ((Q3, gx3, gy3), (Q1, gx1, gy1)):
+            neighbours_inverse(q, gx, gy)
+            zero_missing(gx, gy)
+
+    step(five, 1, *pairs[1], True, True, meanwhile=prepare)
+    step(five, 2, 0.0, 0.0, False, False, meanwhile=lambda: restrict(res, r3, Q5, Q3))
     restrict_face(2, far, r3, Q5, Q3)
     first_update(three, 3, first, True)
-    greeted()
     double_step(three, 3, *pairs, False, False)
     step(three, 5 % SLOTS, 0.0, 0.0, False, False)
     restrict(r3, r1, Q3, Q1)
@@ -987,11 +964,11 @@
             field(6 * 16 * NY), pltpu.VMEM((6, NY, NZ), F32),
             slots(2, Q5 * Q5 * NY), slots(2, Q5 * NY), two(Q5 * Q5 * NY), slots(2, Q5 * NY), pltpu.VMEM((4, 2, NY, NZ), F32),
             slots(4, NY), slots(4, NY), two(Q5 * NY),
-            two(Q3 * Q3 * NY), two(Q1 * Q1 * NY), two(Q3 * NY), two(Q1 * NY), two(Q3 * NY), two(Q1 * NY),
+            two(Q3 * Q3 * NY), two(Q1 * Q1 * NY), two(Q3 * NY), two(Q1 * NY),
             pltpu.VMEM((4, 2, NY, NZ), F32), two(Q5 * Q5 * NY), two(Q5 * NY),
             pltpu.VMEM((4, NY, NZ), F32), two(Q5 * Q5 * NY), two(Q5 * NY),
             dma((2, 4, SLOTS)), dma((2, 4, SLOTS)), dma((2, SLOTS)), dma((2, SLOTS)), dma((4, SLOTS)), dma((4, SLOTS)),
-            dma((4, 3)), dma((4, 3)), dma((8,)), dma((8,)), dma((6,)),
+            dma((8,)), dma((8,)), dma((6,)),
         ],
         compiler_params=pltpu.CompilerParams(
             collective_id=0, has_side_effects=True, vmem_limit_bytes=48 * 2**20

time: 79.1 us -> 77.5 us (0.980); the launches traced: 78.1 us -> 77.3 us
  no operation moved by 1% of the time
where the time goes in v7:
time: 77.5 us; the launch traced here: 77.3 us
  Pallas kernels  76.7 us (99%)
    pallas_call x1, Pallas kernels, per_device(): pl.pallas_call(kernel, out_shape=[jax.ShapeDtypeStruct((n5, NZ), F32)] *...  75.4 us

profile of v7, /device:TPU:13, one launch (start us, length us, event | category | flops | bytes accessed | tf_op | source)
XLA Modules:
  0.0 77.3 jit_solution(11676020947306000638)
XLA Ops:
  0.6 75.4 %shard_map.77 = (f32[1728,128]{1,0:T(8,128)S(1)}, f32[1728,128]{1,0:T(8,128)S(1)}) custom-call(f32[8,128]{1,0:T(8,128)} %bitcast.10, s32[2,8]{1,0:T(2,128)} %bitcast.11, f32[1728,128]{1,0:T(8,128)} %bitcast.9, f32[216,216]{1,0:T(8,128)} %s5_in.1, f32[64,64]{1,0:T(8,128)} %s3_in.1, f32[8,8]{1,0:T(8,128)} %s1_in.1), custom_call_target="tpu_custom_call" | custom-call | tf_op jit(solution)/shard_map/pallas_call | solution.py:951
  76.0 1.3 %shard_map.78 = (f32[1728,128]{1,0:T(8,128)}, f32[1728,128]{1,0:T(8,128)}) custom-call(f32[1728,128]{1,0:T(8,128)S(1)} %get-tuple-element.6.sol, f32[1728,128]{1,0:T(8,128)S(1)} %get-tuple-element.7.res), custom_call_target="tpu_custom_call" | custom-call | tf_op jit(solution)/shard_map/pallas_call | solution.py:985

commit v8 on v7

--- a/solution.py
+++ b/solution.py
@@ -251,7 +251,11 @@
             target[0, pl.ds(i * NY, q), :] = source[pl.ds(i * q * q * NY, q, stride=NY), :]
             target[1, pl.ds(i * NY, q), :] = source[pl.ds((i * q * q + q * (q - 1)) * NY + NY - 1, q, stride=NY), :]
 
-    pack_rows(Q5, res, pack.at[0])
+    for i in range(Q5):
+        for m in range(2):
+            nodes = [i * Q5 * Q5 + m * Q5 * (Q5 - 1) + n for n in range(Q5)]
+            ends_of = [res[pl.ds(node * NY, NY), :][m * (NY - 1) : m * (NY - 1) + 1] for node in nodes]
+            pack[0, m, pl.ds(i * NY, Q5), :] = jnp.concatenate(ends_of, 0)
     pl.semaphore_wait(barrier, sum(there.astype(jnp.int32) for _, there in peers))
 
     def coef_copy(k, arriving):
@@ -956,14 +960,14 @@
         scratch_shapes=[
             two(NY), pltpu.SMEM((2, NY), jnp.int32), pltpu.VMEM((Q5**3, Q5**3), F32), pltpu.VMEM((Q3**3, Q3**3), F32),
             pltpu.SMEM((Q1**3, Q1**3), F32),
-            slots(n5), field(n5), field(n5),
-            field(n3), field(n3), slots(n3), field(n3), field(n3),
-            field(n1), field(n1), slots(n1), field(n1), field(n1),
+            slots(n5 + 16), field(n5), field(n5 + 16),
+            field(n3), field(n3), slots(n3 + 32), field(n3), field(n3 + 32),
+            field(n1), field(n1), slots(n1 + 48), field(n1), field(n1 + 48),
             pltpu.VMEM((224, 224), BF16), pltpu.VMEM((224, 224), BF16),
             pltpu.VMEM((64, 64), BF16), pltpu.VMEM((64, 64), BF16),
             field(6 * 16 * NY), pltpu.VMEM((6, NY, NZ), F32),
-            slots(2, Q5 * Q5 * NY), slots(2, Q5 * NY), two(Q5 * Q5 * NY), slots(2, Q5 * NY), pltpu.VMEM((4, 2, NY, NZ), F32),
-            slots(4, NY), slots(4, NY), two(Q5 * NY),
+            slots(2, Q5 * Q5 * NY), slots(2, Q5 * NY), two(Q5 * Q5 * NY + 24), slots(2, Q5 * NY), pltpu.VMEM((4, 2, NY, NZ), F32),
+            slots(4, NY), slots(4, NY), two(8 * NY),
             two(Q3 * Q3 * NY), two(Q1 * Q1 * NY), two(Q3 * NY), two(Q1 * NY),
             pltpu.VMEM((4, 2, NY, NZ), F32), two(Q5 * Q5 * NY), two(Q5 * NY),
             pltpu.VMEM((4, NY, NZ), F32), two(Q5 * Q5 * NY), two(Q5 * NY),

time: 77.5 us -> 77.5 us (level)
  no operation moved by 1% of the time
where the time goes in v8:
time: 77.5 us; the launch traced here: 77.4 us
  Pallas kernels  76.7 us (99%)
    pallas_call x1, Pallas kernels, per_device(): pl.pallas_call(kernel, out_shape=[jax.ShapeDtypeStruct((n5, NZ), F32)] *...  75.4 us

profile of v8, /device:TPU:13, one launch (start us, length us, event | category | flops | bytes accessed | tf_op | source)
XLA Modules:
  0.0 77.4 jit_solution(1092908465532100971)
XLA Ops:
  0.6 75.4 %shard_map.77 = (f32[1728,128]{1,0:T(8,128)S(1)}, f32[1728,128]{1,0:T(8,128)S(1)}) custom-call(f32[8,128]{1,0:T(8,128)} %bitcast.10, s32[2,8]{1,0:T(2,128)} %bitcast.11, f32[1728,128]{1,0:T(8,128)} %bitcast.9, f32[216,216]{1,0:T(8,128)} %s5_in.1, f32[64,64]{1,0:T(8,128)} %s3_in.1, f32[8,8]{1,0:T(8,128)} %s1_in.1), custom_call_target="tpu_custom_call" | custom-call | tf_op jit(solution)/shard_map/pallas_call | solution.py:955
  76.1 1.3 %shard_map.78 = (f32[1728,128]{1,0:T(8,128)}, f32[1728,128]{1,0:T(8,128)}) custom-call(f32[1728,128]{1,0:T(8,128)S(1)} %get-tuple-element.6.sol, f32[1728,128]{1,0:T(8,128)S(1)} %get-tuple-element.7.res), custom_call_target="tpu_custom_call" | custom-call | tf_op jit(solution)/shard_map/pallas_call | solution.py:989

commit v9 on v8

--- a/solution.py
+++ b/solution.py
@@ -913,8 +913,8 @@
     restrict_face(2, far, r3, Q5, Q3)
     first_update(three, 3, first, True)
     double_step(three, 3, *pairs, False, False)
-    step(three, 5 % SLOTS, 0.0, 0.0, False, False)
-    restrict(r3, r1, Q3, Q1)
+    step(three, 5 % SLOTS, 0.0, 0.0, False, False, meanwhile=lambda: restrict(r3, r1, Q3, Q1))
+    restrict_face(5 % SLOTS, far, r1, Q3, Q1)
     first_update(one, 6 % SLOTS, coarse_first, True)
 
     def coarse_rounds(n, carry):

time: 77.5 us -> 77.5 us (level)
  no operation moved by 1% of the time
where the time goes in v9:
time: 77.5 us; the launch traced here: 77.3 us
  Pallas kernels  76.6 us (99%)
    pallas_call x1, Pallas kernels, per_device(): pl.pallas_call(kernel, out_shape=[jax.ShapeDtypeStruct((n5, NZ), F32)] *...  75.4 us

profile of v9, /device:TPU:13, one launch (start us, length us, event | category | flops | bytes accessed | tf_op | source)
XLA Modules:
  0.0 77.3 jit_solution(7662225934929041853)
XLA Ops:
  0.6 75.4 %shard_map.77 = (f32[1728,128]{1,0:T(8,128)S(1)}, f32[1728,128]{1,0:T(8,128)S(1)}) custom-call(f32[8,128]{1,0:T(8,128)} %bitcast.10, s32[2,8]{1,0:T(2,128)} %bitcast.11, f32[1728,128]{1,0:T(8,128)} %bitcast.9, f32[216,216]{1,0:T(8,128)} %s5_in.1, f32[64,64]{1,0:T(8,128)} %s3_in.1, f32[8,8]{1,0:T(8,128)} %s1_in.1), custom_call_target="tpu_custom_call" | custom-call | tf_op jit(solution)/shard_map/pallas_call | solution.py:955
  76.0 1.3 %shard_map.78 = (f32[1728,128]{1,0:T(8,128)}, f32[1728,128]{1,0:T(8,128)}) custom-call(f32[1728,128]{1,0:T(8,128)S(1)} %get-tuple-element.6.sol, f32[1728,128]{1,0:T(8,128)S(1)} %get-tuple-element.7.res), custom_call_target="tpu_custom_call" | custom-call | tf_op jit(solution)/shard_map/pallas_call | solution.py:989
